TPU v7x, 256 devices: a whole 4x4x8 slice. The times are simulated.
256 devices in a mesh: hist: 32 (over z, x), row: 8 (over y, core).
Axes of the slice: x: 4, y: 4, z: 8, core: 2. Of those that a mesh axis runs over, the one named last changes fastest.
Arguments:
- row_less: float32 [2, 384, 1024], P(None, 'hist'), may hold values from -40 to 40
- row_great: float32 [2, 384, 1024], P(None, 'hist'), may hold values from -5 to 5
- coupling: float32 [32, 32], replicated, may hold values from -1 to 1
- damping: float32 [384, 32], P('hist'), may hold values from 0.2 to 1, as said below
- phases: float32 [384, 32], P('hist'), may hold values from -3.140625 to 3.140625
- lesser_hist: bfloat16 [2, 384, 384, 1024], P(None, 'row', 'hist'), may hold values from -5 to 5
- advanced_hist: bfloat16 [2, 384, 384, 1024], P(None, 'row', 'hist'), may hold values from -5 to 5
- retarded_hist: bfloat16 [2, 384, 384, 1024], P(None, 'row', 'hist'), may hold values from -5 to 5
Outputs:
- stepped_row: float32 [2, 384, 1024], P(None, 'hist')
- column_term: float32 [2, 384, 1024], P(None, 'row')
Inputs may be any that keep to these rules, and one draw needn't show every extreme that they name: `damping`: one-step magnitudes.
All inputs are finite; a program needn't handle non-finite values.
Results may differ from a plain program's by a relative error of at most 0.0029.
Values may be sent and summed in bfloat16 or wider, within the bound.
A program may use at most 128 MiB of HBM per device.

v0:
```python
import jax
import jax.numpy as jnp
from jax import lax
from jax.sharding import PartitionSpec as P


def carried_in(x, axis, combine, identity):
    size, mine = (lax.axis_size(axis), lax.axis_index(axis))
    everything = jax.tree.map(lambda part: lax.all_gather(part, axis), x)
    start = jax.tree.map(
        lambda part, zero: jnp.broadcast_to(jnp.asarray(zero, part.dtype), part.shape), x, identity
    )

    def hop(k, before):
        at = size - 1 - k
        reached = at > mine
        new = combine(before, jax.tree.map(lambda part: part[at], everything))
        return jax.tree.map(lambda a, b: jnp.where(reached, a, b), new, before)

    return lax.fori_loop(0, size, hop, start)


def self_energy(row_less, row_great, coupling):
    steps_here = row_less.shape[1]
    bands = coupling.shape[0]
    less_real = row_less[0].reshape(steps_here, bands, bands)
    less_imag = row_less[1].reshape(steps_here, bands, bands)
    great_real = row_great[0].reshape(steps_here, bands, bands)
    great_imag = row_great[1].reshape(steps_here, bands, bands)
    polar_real = -(less_real * great_real + less_imag * great_imag)
    polar_imag = -(less_imag * great_real - less_real * great_imag)
    highest = lax.Precision.HIGHEST

    def sandwich(polar):
        partial_value = jnp.einsum("ik,skl->sil", coupling, polar, precision=highest)
        return jnp.einsum("sil,jl->sij", partial_value, coupling, precision=highest)

    screen_real = sandwich(polar_real)
    screen_imag = sandwich(polar_imag)
    sigma_less = jnp.stack(
        [
            less_real * screen_real - less_imag * screen_imag,
            less_real * screen_imag + less_imag * screen_real,
        ]
    )
    sigma_great = jnp.stack(
        [
            great_real * screen_real + great_imag * screen_imag,
            great_imag * screen_real - great_real * screen_imag,
        ]
    )
    return ((sigma_great - sigma_less).astype(jnp.bfloat16), sigma_less.astype(jnp.bfloat16))


def contract_row(sigma, hist):
    return jnp.einsum("sik,stkj->tij", sigma, hist, preferred_element_type=jnp.float32)


def contract_column(hist, sigma):
    return jnp.einsum("tsik,sjk->tij", hist, sigma, preferred_element_type=jnp.float32)


def add_pair(earlier, latter):
    return (earlier[0] + latter[0], earlier[1] + latter[1])


def shards(
    row_less, row_great, coupling, damping, phases, lesser_hist, advanced_hist, retarded_hist
):
    bands = coupling.shape[0]
    steps_here = row_less.shape[1]
    rows_here = lesser_hist.shape[1]
    hist_count = lax.axis_size("hist")
    all_steps = steps_here * hist_count
    weight = float(all_steps * bands) ** (-0.5)
    hist_place = lax.axis_index("hist")
    row_place = lax.axis_index("row")
    sigma_ret, sigma_less = self_energy(row_less, row_great, coupling)
    retarded = retarded_hist.reshape(2, rows_here, steps_here, bands, bands)
    later_steps = row_place * rows_here + jnp.arange(rows_here, dtype=jnp.int32)
    earlier_steps = hist_place * steps_here + jnp.arange(steps_here, dtype=jnp.int32)
    causal_column = earlier_steps[None, :] <= later_steps[:, None]
    retarded = jnp.where(
        causal_column[None, :, :, None, None], retarded, jnp.zeros((), jnp.bfloat16)
    )
    column_real = -(
        contract_column(retarded[0], sigma_less[0]) + contract_column(retarded[1], sigma_less[1])
    )
    column_imag = -(
        contract_column(retarded[1], sigma_less[0]) - contract_column(retarded[0], sigma_less[1])
    )
    column_part = weight * jnp.stack([column_real, column_imag]).reshape(
        2, rows_here, bands * bands
    )
    stacked = jnp.stack([sigma_ret, sigma_less]).reshape(2, 2, steps_here, bands * bands)
    whole_row = lax.all_gather(stacked, "hist", axis=2, tiled=True)
    nearby = lax.dynamic_slice_in_dim(whole_row, row_place * rows_here, rows_here, 2)
    nearby = nearby.reshape(2, 2, rows_here, bands, bands)
    near_ret = nearby[0]
    near_less = nearby[1]
    lesser = lesser_hist.reshape(2, rows_here, steps_here, bands, bands)
    summed_steps = row_place * rows_here + jnp.arange(rows_here, dtype=jnp.int32)
    target_steps = hist_place * steps_here + jnp.arange(steps_here, dtype=jnp.int32)
    causal_row = summed_steps[:, None] <= target_steps[None, :]
    advanced = jnp.where(
        causal_row[None, :, :, None, None],
        advanced_hist.reshape(2, rows_here, steps_here, bands, bands),
        jnp.zeros((), jnp.bfloat16),
    )
    real_part = (
        contract_row(near_ret[0], lesser[0])
        - contract_row(near_ret[1], lesser[1])
        + contract_row(near_less[0], advanced[0])
        - contract_row(near_less[1], advanced[1])
    )
    imag_part = (
        contract_row(near_ret[0], lesser[1])
        + contract_row(near_ret[1], lesser[0])
        + contract_row(near_less[0], advanced[1])
        + contract_row(near_less[1], advanced[0])
    )
    partial_row = weight * jnp.stack([real_part, imag_part]).reshape(2, steps_here, bands * bands)
    log_rate = jnp.log(damping)
    inner_log = jnp.cumsum(log_rate[::-1], axis=0)[::-1]
    inner_phase = jnp.cumsum(phases[::-1], axis=0)[::-1]
    zero_row = jnp.zeros((bands,), jnp.float32)
    above_log, above_phase = carried_in(
        (inner_log[0], inner_phase[0]), "hist", add_pair, (zero_row, zero_row)
    )
    summed_log = inner_log + above_log[None, :]
    summed_phase = inner_phase + above_phase[None, :]
    magnitude = jnp.exp(summed_log)
    factor_real = jnp.repeat(magnitude * jnp.cos(summed_phase), bands, axis=1)
    factor_imag = jnp.repeat(-magnitude * jnp.sin(summed_phase), bands, axis=1)
    collision = lax.psum(partial_row, "row")
    sum_real = row_less[0] + collision[0]
    sum_imag = row_less[1] + collision[1]
    stepped_real = factor_real * sum_real - factor_imag * sum_imag
    stepped_imag = factor_real * sum_imag + factor_imag * sum_real
    local_squares = jnp.sum(stepped_real * stepped_real) + jnp.sum(stepped_imag * stepped_imag)
    squares = lax.psum(local_squares, "hist")
    column_term = lax.psum(column_part, "hist")
    norm_scale = jnp.sqrt(squares / (2 * all_steps * bands * bands) + 1e-06)
    stepped_row = jnp.stack([stepped_real, stepped_imag]) / norm_scale
    return (stepped_row, column_term)


def solution(mesh):
    return jax.shard_map(
        shards,
        mesh=mesh,
        in_specs=(
            P(None, "hist", None),
            P(None, "hist", None),
            P(),
            P("hist", None),
            P("hist", None),
            P(None, "row", "hist", None),
            P(None, "row", "hist", None),
            P(None, "row", "hist", None),
        ),
        out_specs=(P(None, "hist", None), P(None, "row", None)),
        check_vma=False,
    )
```

profile of v0, /device:TPU:1, one launch (start us, length us, event | category | flops | bytes accessed | tf_op | source)
XLA Modules:
  0.0 347.8 jit_solution(17631460539322605690)
XLA Ops:
  16.7 4.6 %copy.78 = bf16[2,48,12,1024]{1,3,2,0:T(8,128)(2,1)} copy(bf16[2,48,12,1024]{3,1,2,0:T(8,128)(2,1)S(1)} %copy-done.3) | data formatting | bytes 4718592 | tf_op args[6]
  21.3 6.4 %copy.87 = bf16[2,48,12,1024]{1,3,2,0:T(8,128)(2,1)} copy(bf16[2,48,12,1024]{3,1,2,0:T(8,128)(2,1)} %param.17) | data formatting | bytes 4718592 | tf_op args[7]
  27.8 8.2 %broadcast_select_fusion.4 = (bf16[2,48,12,32,32]{1,4,3,2,0:T(8,128)(2,1)S(1)}, bf16[2,48,12,32,32]{1,4,3,2,0:T(8,128)(2,1)}) fusion(bf16[2,48,12,32,32]{1,4,3,2,0:T(8,128)(2,1)} %bitcast.188, pred[48,12]{0,1:T(8,128)(4,1)S(1)} %get-tuple-element.226, bf16[2,48,12,32,32]{1,4,3,2,0:T(8,128)(2,1)} %bitcast.187, pred[48,12]{0,1:T(8,128)(4,1)S(1)} %get-tuple-element.227), kind=kLoop, calls=%fused_computation.4 | loop fusion | flops 2359296 | bytes 9438336 | tf_op jit(solution)/shard_map/jit(_where)/select_n | solution.py:83
  36.8 1.8 copy-done.2
  39.6 2.8 fusion.8
  42.5 2.7 fusion.15
  46.0 1.9 fusion.55
  47.9 4.8 %squeeze.77 = bf16[48,12,32,32]{3,2,0,1:T(8,128)(2,1)} reshape(bf16[1,48,12,1024]{3,1,2,0:T(8,128)(2,1)S(1)} %get-tuple-element.210) | data formatting | bytes 2359296 | tf_op jit(solution)/shard_map/squeeze | solution.py:112
  52.7 4.8 %squeeze.75 = bf16[48,12,32,32]{3,2,0,1:T(8,128)(2,1)} reshape(bf16[1,48,12,1024]{3,1,2,0:T(8,128)(2,1)S(1)} %get-tuple-element.211) | data formatting | bytes 2359296 | tf_op jit(solution)/shard_map/squeeze | solution.py:111
  57.5 39.1 %all-gather.4.cloned.1.call-done = bf16[2,2,384,1024]{3,1,0,2:T(2,128)(2,1)} async-done(((bf16[2,2,12,1024]{3,1,0,2:T(2,128)(2,1)}), bf16[2,2,384,1024]{3,1,0,2:T(2,128)(2,1)}) %all-gather.4.cloned.1.call-update) | async-done | bytes 3145744 | tf_op jit(solution)/shard_map/all_gather | solution.py:96
  96.6 4.0 %dynamic-slice_reduce_fusion = (bf16[48,1024]{1,0:T(8,128)(2,1)S(1)}, bf16[48,1024]{1,0:T(8,128)(2,1)}, bf16[48,1024]{1,0:T(8,128)(2,1)S(1)}, bf16[48,1024]{1,0:T(8,128)(2,1)S(1)}) fusion(bf16[2,2,384,1024]{3,1,0,2:T(2,128)(2,1)} %all-gather.4.cloned.1.call-done, s32[]{:T(128)S(6)} %add.190, s32[]{:T(128)S(6)} %select_n.54), kind=kLoop, calls=%fused_computation.49 | loop fusion | bytes 786440 | tf_op jit(solution)/shard_map/slice | solution.py:114
  105.2 3.7 %convolution_bitcast_fusion.2 = f32[32,12,32]{2,0,1:T(8,128)S(1)} fusion(bf16[48,32,32,1]{2,1,0,3:T(8,128)(2,1)S(1)} %reshape.261, bf16[48,12,32,32]{3,2,0,1:T(8,128)(2,1)} %squeeze.77), kind=kOutput, calls=%fused_computation.28 | convolution fusion | flops 37748736 | bytes 1327104 | tf_op jit(solution)/shard_map/sik,stkj->tij/dot_general | solution.py:56
  110.5 2.4 fusion.16
  114.2 3.1 fusion.22
  118.5 3.7 %fusion.27 = f32[12,32,32]{2,1,0:T(8,128)S(1)} fusion(f32[32,12,32]{2,0,1:T(8,128)S(1)} %convolution_bitcast_fusion, bf16[48,32,32,1]{2,1,0,3:T(8,128)(2,1)S(1)} %reshape.259, bf16[48,12,32,32]{3,2,0,1:T(8,128)(2,1)} %squeeze.77), kind=kOutput, calls=%fused_computation.43 | convolution fusion | flops 37761024 | bytes 1376256 | tf_op jit(solution)/shard_map/sik,stkj->tij/dot_general | solution.py:56
  122.2 4.4 %fusion.23 = f32[12,32,32]{2,1,0:T(8,128)S(1)} fusion(f32[12,32,32]{2,1,0:T(8,128)S(1)} %fusion.27, bf16[2,48,12,32,32]{1,4,3,2,0:T(8,128)(2,1)} %get-tuple-element.229, bf16[48,32,32]{0,1,2:T(8,128)(2,1)S(1)} %copy-done.15), kind=kOutput, calls=%fused_computation.39 | convolution fusion | flops 37761024 | bytes 3342336 | tf_op jit(solution)/shard_map/sik,stkj->tij/dot_general | solution.py:56
  126.7 2.4 fusion.20
  131.0 30.1 %all-gather = f32[32,1,32]{2,1,0:T(1,128)S(1)} all-gather(f32[1,1,32]{2,1,0:T(1,128)S(1)} %slice_bitcast_fusion.45), channel_id=1, replica_groups=mesh['hist'=32,'row'=8] {'hist'}, dimensions={0}, use_global_device_ids=true | all-gather | bytes 4224 | tf_op jit(solution)/shard_map/all_gather | solution.py:9
  161.1 28.8 %all-gather.1 = f32[32,1,32]{2,1,0:T(1,128)S(1)} all-gather(f32[1,1,32]{2,1,0:T(1,128)S(1)} %slice_bitcast_fusion.44), channel_id=1, replica_groups=mesh['hist'=32,'row'=8] {'hist'}, dimensions={0}, use_global_device_ids=true | all-gather | bytes 4224 | tf_op jit(solution)/shard_map/all_gather | solution.py:9
  189.9 1.6 while.18
  193.2 1.6 multiply_reduce_fusion.1
  196.0 62.1 %psum.22 = f32[]{:T(128)} all-reduce(f32[]{:T(128)S(6)} %add.177), channel_id=1, replica_groups=mesh['hist'=32,'row'=8] {'hist'}, use_global_device_ids=true, to_apply=%region_7.8 | all-reduce | flops 1 | bytes 8 | tf_op jit(solution)/shard_map/psum | solution.py:141
  259.5 79.9 %all-reduce.5.cloned.1.call-done = f32[2,48,1024]{2,1,0:T(8,128)} async-done(((f32[2,48,1024]{2,1,0:T(8,128)}), f32[2,48,1024]{2,1,0:T(8,128)}) %all-reduce.5.cloned.1.call-update) | async-done | bytes 393232 | tf_op jit(solution)/shard_map/psum | solution.py:142
  339.5 1.8 copy.131
  (142 shorter events, 25.7 us)
Async XLA Ops:
  7.2 3.6 %copy-start = (f32[32,32]{1,0:T(8,128)S(1)}, f32[32,32]{1,0:T(8,128)}, u32[]{:S(2)}) copy-start(f32[32,32]{1,0:T(8,128)} %param.12) | copy-start | bytes 12292
  7.2 9.6 %copy-start.3 = (bf16[2,48,12,1024]{3,1,2,0:T(8,128)(2,1)S(1)}, bf16[2,48,12,1024]{3,1,2,0:T(8,128)(2,1)}, u32[]{:S(2)}) copy-start(bf16[2,48,12,1024]{3,1,2,0:T(8,128)(2,1)} %param.16) | copy-start | bytes 7077892
  7.2 89.4 %all-gather.4.cloned.1.call-start = ((), (), s32[]{:S(2)}) async-start(), calls=%async_computation | async-start | bytes 3244032 | tf_op jit(solution)/shard_map/all_gather | solution.py:96
  8.4 0.7 copy-start.10
  13.5 22.5 %copy-start.5 = (f32[12,32,32]{2,1,0:T(8,128)}, f32[12,32,32]{2,1,0:T(8,128)S(1)}, u32[]{:S(2)}) copy-start(f32[12,32,32]{2,1,0:T(8,128)S(1)} %get-tuple-element.217) | copy-start | bytes 147460
  13.5 23.3 %copy-start.7 = (f32[12,32,32]{2,1,0:T(8,128)}, f32[12,32,32]{2,1,0:T(8,128)S(1)}, u32[]{:S(2)}) copy-start(f32[12,32,32]{2,1,0:T(8,128)S(1)} %get-tuple-element.216) | copy-start | bytes 147460
  16.7 176.5 %all-reduce.3.cloned.1.call-start = ((), (), s32[]{:S(2)}) async-start(), calls=%async_computation.1 | async-start | bytes 262144 | tf_op jit(solution)/shard_map/psum | solution.py:135
  36.0 2.6 copy-start.2
  38.6 3.8 %copy-start.6 = (f32[12,32,32]{2,1,0:T(8,128)S(1)}, f32[12,32,32]{2,1,0:T(8,128)}, u32[]{:S(2)}) copy-start(f32[12,32,32]{2,1,0:T(8,128)} %copy-done.5) | copy-start | bytes 147460
  100.8 9.3 %slice-start = ((s8[6291456]{0:T(1024)(128)(4,1)}), s8[2097152]{0:T(1024)(128)(4,1)S(1)}, s32[]{:S(2)}) async-start(s8[6291456]{0:T(1024)(128)(4,1)} %bitcast.189), calls=%async_computation.3 | async-start | bytes 4194304
  105.2 3.8 %copy-start.1 = (bf16[48,12,32,32]{3,2,0,1:T(8,128)(2,1)S(1)}, bf16[48,12,32,32]{3,2,0,1:T(8,128)(2,1)}, u32[]{:S(2)}) copy-start(bf16[48,12,32,32]{3,2,0,1:T(8,128)(2,1)} %squeeze.75) | copy-start | bytes 3538948
  105.2 5.0 %slice-start.1 = ((s8[6291456]{0:T(1024)(128)(4,1)}), s8[4194304]{0:T(1024)(128)(4,1)S(1)}, s32[]{:S(2)}) async-start(s8[6291456]{0:T(1024)(128)(4,1)} %bitcast.189), calls=%async_computation.4 | async-start | bytes 8388608
  109.0 1.5 copy-start.12
  112.9 1.2 copy-start.14
  117.3 9.3 %slice-start.2 = ((s8[6291456]{0:T(1024)(128)(4,1)}), s8[2097152]{0:T(1024)(128)(4,1)S(1)}, s32[]{:S(2)}) async-start(s8[6291456]{0:T(1024)(128)(4,1)} %bitcast.191), calls=%async_computation.5 | async-start | bytes 4194304
  118.5 3.7 %copy-start.15 = (bf16[48,32,32]{0,1,2:T(8,128)(2,1)S(1)}, bf16[48,32,32]{0,1,2:T(8,128)(2,1)}, u32[]{:S(2)}) copy-start(bf16[48,32,32]{0,1,2:T(8,128)(2,1)} %copy.79) | copy-start | bytes 294916
  118.5 8.1 %slice-start.3 = ((s8[6291456]{0:T(1024)(128)(4,1)}), s8[4194304]{0:T(1024)(128)(4,1)S(1)}, s32[]{:S(2)}) async-start(s8[6291456]{0:T(1024)(128)(4,1)} %bitcast.191), calls=%async_computation.6 | async-start | bytes 8388608
  118.5 8.1 %copy-start.13 = (bf16[48,32,32]{0,1,2:T(8,128)(2,1)S(1)}, bf16[48,32,32]{0,1,2:T(8,128)(2,1)}, u32[]{:S(2)}) copy-start(bf16[48,32,32]{0,1,2:T(8,128)(2,1)} %copy.81) | copy-start | bytes 294916
  122.2 7.8 %copy-start.4 = (f32[1,48,1024]{2,1,0:T(8,128)S(1)}, f32[1,48,1024]{2,1,0:T(8,128)}, u32[]{:S(2)}) copy-start(f32[1,48,1024]{2,1,0:T(8,128)} %copy.89) | copy-start | bytes 589828
  126.6 4.2 %copy-start.16 = (f32[12,32]{1,0:T(8,128)S(1)}, f32[12,32]{1,0:T(8,128)}, u32[]{:S(2)}) copy-start(f32[12,32]{1,0:T(8,128)} %param.13) | copy-start | bytes 4612
  126.7 4.3 %copy-start.17 = (f32[12,32]{1,0:T(8,128)S(1)}, f32[12,32]{1,0:T(8,128)}, u32[]{:S(2)}) copy-start(f32[12,32]{1,0:T(8,128)} %param.14) | copy-start | bytes 4612
  126.7 66.5 %copy-start.9 = (f32[1,12,1024]{2,0,1:T(1,128)S(1)}, f32[1,12,1024]{2,0,1:T(1,128)}, u32[]{:S(2)}) copy-start(f32[1,12,1024]{2,0,1:T(1,128)} %copy-done.8) | copy-start | bytes 147460
  126.7 66.5 %copy-start.11 = (f32[1,12,1024]{2,0,1:T(1,128)S(1)}, f32[1,12,1024]{2,0,1:T(1,128)}, u32[]{:S(2)}) copy-start(f32[1,12,1024]{2,0,1:T(1,128)} %copy-done.10) | copy-start | bytes 147460
  130.0 209.5 %all-reduce.5.cloned.1.call-start = ((), (), s32[]{:S(2)}) async-start(), calls=%async_computation.2 | async-start | bytes 786432 | tf_op jit(solution)/shard_map/psum | solution.py:142
  (1 other events, 0.6 us)
Sparse Core Ops, SparseCore 0:
  16.8 79.7 all-gather.3
  130.1 63.0 all-reduce.2
  197.6 141.8 all-reduce.4
where the time goes:
time: 352 us; the launch traced here: 348 us
  blocking collectives  121 us (34%)
  waiting for transfers between devices  120 us (34%)
  local copies, waits for them, and re-layouts  45.4 us (13%)
  matrix products  31.9 us (9%)
  between operations  16.1 us (5%)
  other arithmetic  12 us (3%)
    psum x1, waiting for transfers between devices, shards(): column_term = lax.psum(column_part, 'hist')  79.9 us
    psum x1, blocking collectives, shards(): squares = lax.psum(local_squares, 'hist')  62.1 us
    all_gather x2, blocking collectives, carried_in(): everything = jax.tree.map(lambda part: lax.all_gather(part, axis), x)  58.9 us
    all_gather x1, waiting for transfers between devices, shards(): whole_row = lax.all_gather(stacked, 'hist', axis=2, tiled=True)  39.1 us
    dot_general x8, matrix products, contract_row(): jnp.einsum('sik,stkj->tij', sigma, hist, preferred_element_type=jnp.float32)  22.1 us
    unnamed x53, local copies, waits for them, and re-layouts  16.5 us
    select_n x1, other arithmetic, shards(): jnp.where(causal_column[None, :, :, None, None], retarded, jnp.zeros((),...  8.16 us
    dot_general x4, matrix products, contract_column(): jnp.einsum('tsik,sjk->tij', hist, sigma, preferred_element_type=jnp.float32)  7.14 us
  transfers between devices with their start and end apart: 3, of which 3 were waited for; matrix products, arithmetic and copies ran while one was open for 12% of the time, Pallas kernels for 0%

commit v1 on v0

v1 whole, which is shorter than its diff:
```python
import functools

import jax
import jax.numpy as jnp
import numpy as np
from jax import lax
from jax.experimental import pallas as pl
from jax.experimental.pallas import tpu as pltpu
from jax.sharding import PartitionSpec as P

MESH = pl.DeviceIdType.MESH
F32 = jnp.float32
BF16 = jnp.bfloat16
HIGHEST = lax.Precision.HIGHEST
NX = 4
NZ = 8
NR = 8
TP = 12
TR = 48
OWNERS = 6
LANES_TO_LANES = (((1,), (1,)), ((), ()))


def lane_order():
    one = np.zeros((TP * 32, 4 * 128), np.float32)
    two = np.zeros((NX * 128, 8 * TR), np.float32)
    for s in range(TP):
        for c in range(8):
            for q in range(4):
                one[s * 32 + 4 * c + q, q * 128 + c * TP + s] = 1
            for x in range(NX):
                two[x * 128 + c * TP + s, c * TR + x * TP + s] = 1
    three = np.zeros((128, 128), np.float32)
    for q in range(4):
        for a in range(4):
            for c in range(8):
                three[q * 32 + a * 8 + c, q * 32 + 4 * c + a] = 1
    return one, two, three


def body(
    x_hbm, y_hbm, c_hbm, damp_hbm, phase_hbm, les_hbm, adv_hbm, ret_hbm, one_hbm, two_hbm, three_hbm,
    out_ref, col_ref,
    xv, yv, cv, dampv, phasev, lesv, advv, retv, onev, twov, threev,
    sig_own, sig_all, bmat, col_acc, col_send, col_x, colz_send, col_z, col_own, col_all,
    lmat, fpart, rs_buf, ag_buf, tot_x, tot_z, nrm_x, nrm_z, facv, stepv,
    load_sem, send_sem, recv_sem,
):
    h = lax.axis_index("hist")
    r = lax.axis_index("row")
    z, x = h // NX, h % NX
    dz = (z - r + NZ) % NZ
    early = z <= r
    late = z >= r

    def at_x(d):
        return {"hist": z * NX + (x + d) % NX}

    def at_z(d):
        return {"hist": ((z + d + NZ) % NZ) * NX + x}

    def at_r(d):
        return {"row": (r + d) % NR}

    counts = {"send": 0, "recv": 0}
    pending = []

    def slots(kind, n):
        first = counts[kind]
        counts[kind] += n
        return first

    def copy(src, dst, send, recv, device):
        return pltpu.make_async_remote_copy(
            src_ref=src, dst_ref=dst, send_sem=send_sem.at[send], recv_sem=recv_sem.at[recv],
            device_id=device, device_id_type=MESH,
        )

    def start(cond, *args):
        if cond is None:
            copy(*args).start()
        else:
            @pl.when(cond)
            def _():
                copy(*args).start()
        pending.append((cond, args))

    def arrived(ref, recv):
        copy(ref, ref, 0, recv, at_x(1)).wait_recv()

    loads = []
    for src, dst in (
        (c_hbm, cv), (x_hbm, xv), (y_hbm, yv), (damp_hbm, dampv), (phase_hbm, phasev),
        (one_hbm, onev), (two_hbm, twov), (three_hbm, threev), (ret_hbm, retv), (les_hbm, lesv), (adv_hbm, advv),
    ):
        loads.append(pltpu.make_async_copy(src, dst, load_sem.at[len(loads)]))
        loads[-1].start()
    (c_load, x_load, y_load, damp_load, phase_load, one_load, two_load, three_load, ret_load, les_load, adv_load) = loads

    barrier = pltpu.get_barrier_semaphore()
    for d in range(1, NX):
        pl.semaphore_signal(barrier, inc=1, device_id=at_x(d), device_id_type=MESH)
    for d in range(1, NZ):
        pl.semaphore_signal(barrier, inc=1, device_id=at_z(d), device_id_type=MESH)
    for d in range(1, NR):
        pl.semaphore_signal(barrier, inc=1, device_id=at_r(d), device_id_type=MESH)

    lane8 = lax.broadcasted_iota(jnp.int32, (8, 128), 1) // 32

    def by_group(parts):
        mask = lane8.reshape((1,) * (parts[0].ndim - 2) + (8, 128))
        out = parts[0]
        for g in range(1, 4):
            out = jnp.where(mask == g, parts[g], out)
        return out

    def rolled(a):
        flat = a.reshape(-1, 128)
        return [a] + [pltpu.roll(flat, 32 * d, 1).reshape(a.shape) for d in range(1, 4)]

    c_load.wait()
    coup = cv[...]
    wide = jnp.concatenate([coup] * 4, axis=1)
    square = jnp.concatenate([wide] * 4, axis=0)
    same = (
        lax.broadcasted_iota(jnp.int32, (128, 128), 0) // 32
        == lax.broadcasted_iota(jnp.int32, (128, 128), 1) // 32
    )
    right = jnp.where(same, square, 0.0)
    rows4 = [cv[pl.ds(g, 8, stride=4), :] for g in range(4)]
    col_of = [[jnp.broadcast_to(rows4[g][:, k : k + 1], (8, 128)) for k in range(32)] for g in range(4)]

    x_load.wait()
    y_load.wait()

    def part(ref, p):
        return ref[pl.ds(p, TP * 8, stride=2), :]

    xr, xi, yr, yi = part(xv, 0), part(xv, 1), part(yv, 0), part(yv, 1)
    polar = jnp.concatenate([-(xr * yr + xi * yi), -(xi * yr - xr * yi)], axis=0)
    half = lax.dot_general(polar, right, LANES_TO_LANES, precision=HIGHEST, preferred_element_type=F32)
    half = half.reshape(2 * TP, 8, 128)
    half_d = rolled(half)
    screen = jnp.zeros((2 * TP, 8, 128), F32)
    for d in range(4):
        for c in range(8):
            factor = by_group([col_of[g][4 * c + (g - d) % 4] for g in range(4)])
            screen = screen + factor[None] * half_d[d][:, c : c + 1, :]
    sr, si = screen[:TP], screen[TP:]
    xr, xi, yr, yi = (a.reshape(TP, 8, 128) for a in (xr, xi, yr, yi))
    less = (xr * sr - xi * si, xr * si + xi * sr)
    great = (yr * sr + yi * si, yi * sr - yr * si)
    ret = (great[0] - less[0], great[1] - less[1])
    less_d = [rolled(a) for a in less]
    for a, pair in enumerate(([rolled(v) for v in ret], less_d)):
        for p in range(2):
            for m in range(3):
                block = jnp.concatenate(
                    [by_group([pair[p][(g - b) % 4][4 * m + g] for g in range(4)]) for b in range(4)], axis=0
                )
                sig_own[a, pl.ds(p * 32, 32), pl.ds(m * 128, 128)] = block.astype(BF16)

    damp_load.wait()
    phase_load.wait()
    logs = jnp.concatenate([jnp.log(dampv[...]), phasev[...]], axis=1)
    tot = jnp.sum(logs, axis=0, keepdims=True)
    tot = jnp.concatenate([tot, jnp.zeros((1, 64), F32)], axis=1)
    tot_x[x] = jnp.broadcast_to(tot, (8, 128))

    pl.semaphore_wait(barrier, (NX - 1) + (NZ - 1) + (NR - 1))

    source = dz == 0
    up = (dz == 1) | (dz == 2) | (dz == 3)
    down = (dz == 7) | (dz == 6)
    z_send, z_recv = slots("send", 4), slots("recv", 2)
    f_send = slots("send", 4)
    sx_send, sx_recv = slots("send", 6), slots("recv", 6)
    for a in range(2):
        start(source, sig_own.at[a], sig_all.at[a, x], z_send + 2 * a, z_recv + a, at_z(1))
        start(source, sig_own.at[a], sig_all.at[a, x], z_send + 2 * a + 1, z_recv + a, at_z(-1))

    @pl.when(source)
    def _():
        sig_all[:, x] = sig_own[...]

    tx_send, tx_recv = slots("send", 3), slots("recv", 3)
    for d in range(1, NX):
        start(None, tot_x.at[x], tot_x.at[x], tx_send + d - 1, tx_recv + d - 1, at_x(d))

    @pl.when(early)
    def _():
        def square_of(p, s):
            rows = []
            for g in range(4):
                for b in range(4):
                    rows.append(jnp.where(lane8 == g, less_d[p][(g - b) % 4][s], 0.0))
            return jnp.concatenate(rows, axis=0)

        for s in range(TP):
            b0, b1 = square_of(0, s), square_of(1, s)
            bmat[s, pl.ds(0, 128), pl.ds(0, 128)] = b0.astype(BF16)
            bmat[s, pl.ds(0, 128), pl.ds(128, 128)] = b1.astype(BF16)
            bmat[s, pl.ds(128, 128), pl.ds(0, 128)] = (-b1).astype(BF16)
            bmat[s, pl.ds(128, 128), pl.ds(128, 128)] = b0.astype(BF16)

    for a in range(2):
        @pl.when(jnp.logical_not(source))
        def _():
            arrived(sig_own.at[a], z_recv + a)

        start(up, sig_all.at[a, x], sig_all.at[a, x], f_send + 2 * a, z_recv + a, at_z(1))
        start(down, sig_all.at[a, x], sig_all.at[a, x], f_send + 2 * a + 1, z_recv + a, at_z(-1))
        for d in range(1, NX):
            start(
                None if a == 0 else late, sig_all.at[a, x], sig_all.at[a, x],
                sx_send + 3 * a + d - 1, sx_recv + 3 * a + d - 1, at_x(d),
            )

    tz_send, tz_recv = slots("send", 7), slots("recv", 7)
    for d in range(1, NX):
        arrived(tot_x.at[0], tx_recv + d - 1)
    tot_z[z] = tot_x[0] + tot_x[1] + tot_x[2] + tot_x[3]
    for d in range(1, NZ):
        start(None, tot_z.at[z], tot_z.at[z], tz_send + d - 1, tz_recv + d - 1, at_z(d))

    weight = float(NX * NZ * TP * 32) ** -0.5
    ret_load.wait()
    three_load.wait()
    cx_send, cx_recv = slots("send", 3), slots("recv", 3)

    @pl.when(early)
    def _():
        t_row = lax.broadcasted_iota(jnp.int32, (TR, 128), 0)
        col_acc[...] = jnp.zeros_like(col_acc)

        def step(s, carry):
            keep = t_row >= h * TP + s - r * TR
            rows = [
                jnp.concatenate(
                    [jnp.where(keep, retv[p, s, :, pl.ds(c * 128, 128)], jnp.zeros((), BF16)) for p in range(2)], axis=1
                )
                for c in range(8)
            ]
            col_acc[...] += lax.dot_general(
                jnp.concatenate(rows, axis=0), bmat[s], LANES_TO_LANES, preferred_element_type=F32
            )
            return carry

        lax.fori_loop(0, TP, step, 0)
        for c in range(8):
            for po in range(2):
                value = (col_acc[pl.ds(c * TR, TR), pl.ds(po * 128, 128)] * -weight).astype(BF16)
                value = jnp.dot(value, threev[...], preferred_element_type=F32)
                col_send[c // 2, pl.ds(((c % 2) * 2 + po) * TR, TR), :] = value.astype(BF16)

    for d in range(1, NX):
        start(early, col_send.at[(x + d) % NX], col_x.at[d - 1], cx_send + d - 1, cx_recv + d - 1, at_x(d))

    one_load.wait()
    two_load.wait()

    def left_matrix(a):
        blocks = [
            jnp.dot(sig_all[a, j], onev[...], preferred_element_type=F32).astype(BF16) for j in range(NX)
        ]
        parts = []
        for p in range(2):
            gathered = jnp.concatenate(
                [
                    jnp.concatenate([b[p * 32 : p * 32 + 32, q * 128 : q * 128 + 128] for b in blocks], axis=1)
                    for q in range(4)
                ],
                axis=0,
            )
            parts.append(jnp.dot(gathered, twov[...], preferred_element_type=F32))
        lmat[pl.ds(0, 128), pl.ds(0, 384)] = parts[0].astype(BF16)
        lmat[pl.ds(0, 128), pl.ds(384, 384)] = (-parts[1]).astype(BF16)
        lmat[pl.ds(128, 128), pl.ds(0, 384)] = parts[1].astype(BF16)
        lmat[pl.ds(128, 128), pl.ds(384, 384)] = parts[0].astype(BF16)

    s_row = lax.broadcasted_iota(jnp.int32, (TR, 128), 0)

    def contract(ref, masked):
        def step(pair, carry):
            cols = []
            for j in range(2):
                t = pair * 2 + j
                blocks = [ref[p, t, :, pl.ds(c * 128, 128)] for p in range(2) for c in range(8)]
                if masked:
                    keep = s_row <= h * TP + t - r * TR
                    blocks = [jnp.where(keep, b, jnp.zeros((), BF16)) for b in blocks]
                cols.append(jnp.concatenate(blocks, axis=0))
            out = jnp.dot(lmat[...], jnp.concatenate(cols, axis=1), preferred_element_type=F32) * weight
            for j in range(2):
                for po in range(2):
                    def block(q, b):
                        first = po * 128 + q * 32 + b * 8
                        return out[first : first + 8, j * 128 : j * 128 + 128]

                    total = by_group([block(q, q) for q in range(4)])
                    for d in range(1, 4):
                        moved = by_group([block(q, (q + d) % 4) for q in range(4)])
                        total = total + pltpu.roll(moved, 32 * d, 1)
                    at = (pair * 2 + j) * 2 + po
                    if masked:
                        fpart[at] += total
                    else:
                        fpart[at] = total
            return carry

        lax.fori_loop(0, TP // 2, step, 0)

    les_load.wait()
    for d in range(1, NX):
        arrived(sig_own.at[0], sx_recv + d - 1)
    left_matrix(0)
    contract(lesv, False)
    adv_load.wait()

    @pl.when(late)
    def _():
        for d in range(1, NX):
            arrived(sig_own.at[1], sx_recv + 3 + d - 1)
        left_matrix(1)
        contract(advv, True)

    rs_send, rs_recv = slots("send", 7), slots("recv", 7)
    for d in range(1, NR):
        start(None, fpart.at[pl.ds(3 * ((r + d) % NR), 3)], rs_buf.at[d - 1], rs_send + d - 1, rs_recv + d - 1, at_r(d))

    cz_send, cz_recv = slots("send", 7), slots("recv", 7)

    @pl.when(early)
    def _():
        for d in range(1, NX):
            arrived(col_x.at[d - 1], cx_recv + d - 1)
        total = col_send[x].astype(F32)
        for d in range(1, NX):
            total = total + col_x[d - 1].astype(F32)
        for j in range(OWNERS):
            colz_send[j] = total[j * 32 : j * 32 + 32]

    for d in range(1, NZ):
        to = (z + d) % NZ
        start(
            early & (to < OWNERS), colz_send.at[lax.rem(to, OWNERS)], col_z.at[d - 1], cz_send + d - 1, cz_recv + d - 1, at_z(d)
        )

    for d in range(1, NZ):
        arrived(tot_z.at[0], tz_recv + d - 1)
    above = jnp.zeros((8, 128), F32)
    for j in range(NZ):
        above = above + jnp.where(j > z, tot_z[j], 0.0)
    for j in range(NX):
        above = above + jnp.where(j > x, tot_x[j], 0.0)
    row_i = lax.broadcasted_iota(jnp.int32, (TP, TP), 0)
    later = jnp.where(lax.broadcasted_iota(jnp.int32, (TP, TP), 1) >= row_i, 1.0, 0.0)
    summed = jnp.dot(later, logs, precision=HIGHEST, preferred_element_type=F32) + above[0:1, 0:64]
    magnitude = jnp.exp(summed[:, 0:32])
    angle = summed[:, 32:64]
    factor = jnp.concatenate([magnitude * jnp.cos(angle), -magnitude * jnp.sin(angle)], axis=0)
    spread = jnp.where(
        lax.broadcasted_iota(jnp.int32, (32, 1024), 1) // 32 == lax.broadcasted_iota(jnp.int32, (32, 1024), 0), 1.0, 0.0
    )
    spread = jnp.dot(factor, spread, precision=HIGHEST, preferred_element_type=F32)
    for c in range(8):
        facv[pl.ds(c, 2 * TP, stride=8), :] = spread[:, c * 128 : c * 128 + 128]

    ag_send, ag_recv = slots("send", 7), slots("recv", 7)
    own = fpart[pl.ds(3 * r, 3)]
    for d in range(1, NR):
        arrived(rs_buf.at[d - 1], rs_recv + d - 1)
        own = own + rs_buf[d - 1]
    ag_buf[pl.ds(3 * r, 3)] = own
    for d in range(1, NR):
        start(None, ag_buf.at[pl.ds(3 * r, 3)], ag_buf.at[pl.ds(3 * r, 3)], ag_send + d - 1, ag_recv + d - 1, at_r(d))

    cg_send, cg_recv = slots("send", 7), slots("recv", 7)
    owner = z < OWNERS

    @pl.when(owner)
    def _():
        @pl.when(early)
        def _():
            col_own[...] = colz_send[lax.rem(z, OWNERS)]

        @pl.when(jnp.logical_not(early))
        def _():
            col_own[...] = jnp.zeros_like(col_own)

        for d in range(1, NZ):
            @pl.when((z - d + NZ) % NZ <= r)
            def _():
                arrived(col_z.at[d - 1], cz_recv + d - 1)
                col_own[...] += col_z[d - 1]

        col_all[x, lax.rem(z, OWNERS)] = col_own[...].astype(BF16)

    piece = col_all.at[x, lax.rem(z, OWNERS)]
    for d in range(1, NZ):
        start(owner, piece, piece, cg_send + d - 1, cg_recv + d - 1, at_z(d))

    for d in range(1, NR):
        arrived(rs_buf.at[0], ag_recv + d - 1)
    squares = jnp.zeros((8, 128), F32)
    for t in range(TP):
        fr, fi = facv[pl.ds(t * 8, 8), :], facv[pl.ds((TP + t) * 8, 8), :]
        ar = xv[pl.ds(t * 16, 8, stride=2), :] + ag_buf[2 * t]
        ai = xv[pl.ds(t * 16 + 1, 8, stride=2), :] + ag_buf[2 * t + 1]
        step_r, step_i = fr * ar - fi * ai, fr * ai + fi * ar
        stepv[2 * t] = step_r
        stepv[2 * t + 1] = step_i
        squares = squares + (step_r * step_r + step_i * step_i)
    nrm_x[x] = squares
    nx_send, nx_recv = slots("send", 3), slots("recv", 3)
    for d in range(1, NX):
        start(None, nrm_x.at[x], nrm_x.at[x], nx_send + d - 1, nx_recv + d - 1, at_x(d))

    ca_send, ca_recv = slots("send", 3), slots("recv", 3)
    for d in range(1, NZ):
        @pl.when((z - d + NZ) % NZ < OWNERS)
        def _():
            arrived(col_all.at[0, 0], cg_recv + d - 1)
    for d in range(1, NX):
        start(None, col_all.at[x], col_all.at[x], ca_send + d - 1, ca_recv + d - 1, at_x(d))

    nz_send, nz_recv = slots("send", 7), slots("recv", 7)
    for d in range(1, NX):
        arrived(nrm_x.at[0], nx_recv + d - 1)
    nrm_z[z] = nrm_x[0] + nrm_x[1] + nrm_x[2] + nrm_x[3]
    for d in range(1, NZ):
        start(None, nrm_z.at[z], nrm_z.at[z], nz_send + d - 1, nz_recv + d - 1, at_z(d))
    for d in range(1, NZ):
        arrived(nrm_z.at[0], nz_recv + d - 1)
    total = nrm_z[0]
    for j in range(1, NZ):
        total = total + nrm_z[j]
    total = jnp.sum(jnp.sum(total, axis=0, keepdims=True), axis=1, keepdims=True)
    scale = 1.0 / jnp.sqrt(total / float(2 * NX * NZ * TP * 1024) + 1e-6)
    for t in range(TP):
        out_ref[pl.ds(t * 16, 8, stride=2), :] = stepv[2 * t] * scale
        out_ref[pl.ds(t * 16 + 1, 8, stride=2), :] = stepv[2 * t + 1] * scale

    for d in range(1, NX):
        arrived(col_all.at[0], ca_recv + d - 1)
    col_ref[...] = col_all[...]

    for cond, args in pending:
        if cond is None:
            copy(*args).wait_send()
        else:
            @pl.when(cond)
            def _():
                copy(*args).wait_send()
    assert counts["send"] <= SENDS and counts["recv"] <= RECVS, counts


SENDS = 80
RECVS = 64


def shards(row_less, row_great, coupling, damping, phases, lesser_hist, advanced_hist, retarded_hist):
    def rows(a):
        a = a.transpose(1, 0, 2).reshape(TP, 2, 8, 128)
        return a.transpose(0, 2, 1, 3).reshape(TP * 16, 128)

    one, two, three = (jnp.asarray(m, BF16) for m in lane_order())
    anywhere = pl.BlockSpec(memory_space=pl.ANY)
    vmem = pl.BlockSpec(memory_space=pltpu.VMEM)
    scratch = [
        pltpu.VMEM((TP * 16, 128), F32),
        pltpu.VMEM((TP * 16, 128), F32),
        pltpu.VMEM((32, 32), F32),
        pltpu.VMEM((TP, 32), F32),
        pltpu.VMEM((TP, 32), F32),
        pltpu.VMEM((2, TP, TR, 1024), BF16),
        pltpu.VMEM((2, TP, TR, 1024), BF16),
        pltpu.VMEM((2, TP, TR, 1024), BF16),
        pltpu.VMEM((TP * 32, 512), BF16),
        pltpu.VMEM((NX * 128, 8 * TR), BF16),
        pltpu.VMEM((128, 128), BF16),
        pltpu.VMEM((2, 64, TP * 32), BF16),
        pltpu.VMEM((2, NX, 64, TP * 32), BF16),
        pltpu.VMEM((TP, 256, 256), BF16),
        pltpu.VMEM((8 * TR, 256), F32),
        pltpu.VMEM((NX, 4 * TR, 128), BF16),
        pltpu.VMEM((NX - 1, 4 * TR, 128), BF16),
        pltpu.VMEM((OWNERS, 32, 128), F32),
        pltpu.VMEM((NZ - 1, 32, 128), F32),
        pltpu.VMEM((32, 128), F32),
        pltpu.VMEM((NX, OWNERS, 32, 128), BF16),
        pltpu.VMEM((256, 768), BF16),
        pltpu.VMEM((2 * TP, 8, 128), F32),
        pltpu.VMEM((NR - 1, 3, 8, 128), F32),
        pltpu.VMEM((2 * TP, 8, 128), F32),
        pltpu.VMEM((NX, 8, 128), F32),
        pltpu.VMEM((NZ, 8, 128), F32),
        pltpu.VMEM((NX, 8, 128), F32),
        pltpu.VMEM((NZ, 8, 128), F32),
        pltpu.VMEM((2 * TP * 8, 128), F32),
        pltpu.VMEM((2 * TP, 8, 128), F32),
        pltpu.SemaphoreType.DMA((11,)),
        pltpu.SemaphoreType.DMA((SENDS,)),
        pltpu.SemaphoreType.DMA((RECVS,)),
    ]
    stepped, column = pl.pallas_call(
        body,
        out_shape=(
            jax.ShapeDtypeStruct((TP * 16, 128), F32),
            jax.ShapeDtypeStruct((NX, OWNERS, 32, 128), BF16),
        ),
        in_specs=[anywhere] * 11,
        out_specs=(vmem, vmem),
        scratch_shapes=scratch,
        compiler_params=pltpu.CompilerParams(
            collective_id=0, has_side_effects=True, vmem_limit_bytes=48 * 1024 * 1024
        ),
        name="kadanoff_baym_step",
    )(
        rows(row_less), rows(row_great), coupling, damping, phases,
        lesser_hist.transpose(0, 2, 1, 3), advanced_hist.transpose(0, 2, 1, 3), retarded_hist.transpose(0, 2, 1, 3),
        one, two, three,
    )
    stepped = stepped.reshape(TP, 8, 2, 128).transpose(2, 0, 1, 3).reshape(2, TP, 1024)
    column = column.reshape(NX, 2, 2, TR, 128).transpose(2, 3, 0, 1, 4).reshape(2, TR, 1024)
    return stepped, column.astype(F32)


def solution(mesh):
    return jax.shard_map(
        shards,
        mesh=mesh,
        in_specs=(
            P(None, "hist", None),
            P(None, "hist", None),
            P(),
            P("hist", None),
            P("hist", None),
            P(None, "row", "hist", None),
            P(None, "row", "hist", None),
            P(None, "row", "hist", None),
        ),
        out_specs=(P(None, "hist", None), P(None, "row", None)),
        check_vma=False,
    )
```

time: 352 us -> 61.8 us (0.18); the launches traced: 348 us -> 61.2 us
  blocking collectives: 121 us -> 0 us
  waiting for transfers between devices: 120 us -> 0 us
  Pallas kernels: 0 us -> 48.5 us
  local copies, waits for them, and re-layouts: 45.4 us -> 12 us
  matrix products: 31.9 us -> 0 us
  between operations: 16.1 us -> 0.67 us
  other arithmetic: 12 us -> 0.03 us
    psum x2 -> x0, waiting for transfers between devices: 81.1 us -> none  [the longest x1 79.9 us: shards(): column_term = lax.psum(column_part, 'hist')]
    psum x1 -> x0, blocking collectives: 62.1 us -> none  [shards(): squares = lax.psum(local_squares, 'hist')]
    all_gather x2 -> x0, blocking collectives: 58.9 us -> none  [carried_in(): everything = jax.tree.map(lambda part: lax.all_gather(part, axis), x)]
    pallas_call x0 -> x1, Pallas kernels: none -> 48.5 us  [shards(): pl.pallas_call(body, out_shape=(jax.ShapeDtypeStruct((TP * 16, 128), F32)...]
    all_gather x1 -> x0, waiting for transfers between devices: 39.1 us -> none  [shards(): whole_row = lax.all_gather(stacked, 'hist', axis=2, tiled=True)]
    dot_general x16 -> x0, matrix products: 31.9 us -> none  [the longest x8 22.1 us: contract_row(): jnp.einsum('sik,stkj->tij', sigma, hist, preferred_element_type=jnp.float32)]
    squeeze x8 -> x0, local copies, waits for them, and re-layouts: 14.2 us -> none  [the longest x1 4.8 us: shards(): lesser[1]]
    select_n x33 -> x0, other arithmetic: 8.76 us -> none  [the longest x1 8.16 us: shards(): jnp.where(causal_column[None, :, :, None, None], retarded, jnp.zeros((),...]
  transfers between devices with their start and end apart: 3 -> 0, of which waited for: 3 -> 0; matrix products, arithmetic and copies ran while one was open for 12% -> 0% of each run, Pallas kernels for 0% -> 0%
where the time goes in v1:
time: 61.8 us; the launch traced here: 61.2 us
  Pallas kernels  48.5 us (78%)
  local copies, waits for them, and re-layouts  12 us (19%)
  between operations  0.67 us (1%)
    pallas_call x1, Pallas kernels, shards(): pl.pallas_call(body, out_shape=(jax.ShapeDtypeStruct((TP * 16, 128), F32)...  48.5 us
    unnamed x21, local copies, waits for them, and re-layouts  10.6 us
    convert_element_type x2, local copies, waits for them, and re-layouts, shards(): return (stepped, column.astype(F32))  1.37 us

profile of v1, /device:TPU:1, one launch (start us, length us, event | category | flops | bytes accessed | tf_op | source)
XLA Modules:
  0.0 61.2 jit_solution(8168704814014929511)
XLA Ops:
  0.6 0.0 copy-start
  0.6 1.7 %copy-done = bf16[2,48,12,1024]{3,1,2,0:T(8,128)(2,1)S(1)} copy-done((bf16[2,48,12,1024]{3,1,2,0:T(8,128)(2,1)S(1)}, bf16[2,48,12,1024]{3,1,2,0:T(8,128)(2,1)}, u32[]{:S(2)}) %copy-start) | copy-done | bytes 2359320
  2.3 0.0 copy-start.1
  2.3 1.7 %copy-done.1 = bf16[2,48,12,1024]{3,1,2,0:T(8,128)(2,1)S(1)} copy-done((bf16[2,48,12,1024]{3,1,2,0:T(8,128)(2,1)S(1)}, bf16[2,48,12,1024]{3,1,2,0:T(8,128)(2,1)}, u32[]{:S(2)}) %copy-start.1) | copy-done | bytes 2359320
  4.0 0.0 copy-start.2
  4.0 1.0 %copy-done.2 = bf16[512,384]{1,0:T(8,128)(2,1)S(1)} copy-done((bf16[512,384]{1,0:T(8,128)(2,1)S(1)}, bf16[512,384]{1,0:T(8,128)(2,1)}, u32[]{:S(2)}) %copy-start.2) | copy-done | bytes 393240
  5.0 0.0 copy-start.3
  5.0 1.0 %copy-done.3 = bf16[384,512]{1,0:T(8,128)(2,1)S(1)} copy-done((bf16[384,512]{1,0:T(8,128)(2,1)S(1)}, bf16[384,512]{1,0:T(8,128)(2,1)}, u32[]{:S(2)}) %copy-start.3) | copy-done | bytes 393240
  6.0 0.0 copy-start.4
  6.0 0.9 %copy-done.4 = f32[2,12,1024]{2,0,1:T(2,128)S(1)} copy-done((f32[2,12,1024]{2,0,1:T(2,128)S(1)}, f32[2,12,1024]{2,0,1:T(2,128)}, u32[]{:S(2)}) %copy-start.4) | copy-done | bytes 98328
  6.9 0.0 copy-start.5
  6.9 0.9 %copy-done.5 = f32[2,12,1024]{2,0,1:T(2,128)S(1)} copy-done((f32[2,12,1024]{2,0,1:T(2,128)S(1)}, f32[2,12,1024]{2,0,1:T(2,128)}, u32[]{:S(2)}) %copy-start.5) | copy-done | bytes 98328
  7.7 0.0 copy-start.6
  7.7 0.8 %copy-done.6 = bf16[128,128]{1,0:T(8,128)(2,1)S(1)} copy-done((bf16[128,128]{1,0:T(8,128)(2,1)S(1)}, bf16[128,128]{1,0:T(8,128)(2,1)}, u32[]{:S(2)}) %copy-start.6) | copy-done | bytes 32792
  8.5 0.0 copy-start.7
  8.5 0.7 %copy-done.7 = f32[32,32]{1,0:T(8,128)S(1)} copy-done((f32[32,32]{1,0:T(8,128)S(1)}, f32[32,32]{1,0:T(8,128)}, u32[]{:S(2)}) %copy-start.7) | copy-done | bytes 4120
  9.2 0.0 copy-start.8
  9.2 0.7 %copy-done.8 = f32[12,32]{1,0:T(8,128)S(1)} copy-done((f32[12,32]{1,0:T(8,128)S(1)}, f32[12,32]{1,0:T(8,128)}, u32[]{:S(2)}) %copy-start.8) | copy-done | bytes 1560
  9.9 0.0 copy-start.9
  9.9 0.7 %copy-done.9 = f32[12,32]{1,0:T(8,128)S(1)} copy-done((f32[12,32]{1,0:T(8,128)S(1)}, f32[12,32]{1,0:T(8,128)}, u32[]{:S(2)}) %copy-start.9) | copy-done | bytes 1560
  10.6 48.5 %kadanoff_baym_step.1 = (f32[192,128]{1,0:T(8,128)S(1)}, bf16[4,6,32,128]{3,2,1,0:T(8,128)(2,1)S(1)}) custom-call(f32[192,128]{1,0:T(8,128)S(1)} %bitcast.29, f32[192,128]{1,0:T(8,128)S(1)} %bitcast.30, f32[32,32]{1,0:T(8,128)S(1)} %copy-done.7, f32[12,32]{1,0:T(8,128)S(1)} %copy-done.8, f32[12,32]{1,0:T(8,128)S(1)} %copy-done.9, ...), custom_call_target="tpu_custom_call" | custom-call | tf_op jit(solution)/shard_map/kadanoff_baym_step/pallas_call | solution.py:506
  59.2 0.3 copy.16
  59.5 1.1 %reshape.34 = f32[2,48,1024]{2,1,0:T(8,128)} reshape(f32[2,48,4,2,128]{4,3,2,1,0:T(2,128)S(1)} %copy.16) | data formatting | bytes 786432 | tf_op jit(solution)/shard_map/convert_element_type | solution.py:526
  60.5 0.6 %copy.18 = f32[2,12,1024]{2,0,1:T(2,128)} copy(f32[2,12,1024]{2,0,1:T(2,128)S(1)} %bitcast.31) | data formatting | bytes 196608
  (1 shorter events, 0.0 us)
Async XLA Ops:
  0.6 1.7 %copy-start = (bf16[2,48,12,1024]{3,1,2,0:T(8,128)(2,1)S(1)}, bf16[2,48,12,1024]{3,1,2,0:T(8,128)(2,1)}, u32[]{:S(2)}) copy-start(bf16[2,48,12,1024]{3,1,2,0:T(8,128)(2,1)} %param.16) | copy-start | bytes 7077892
  2.3 1.7 %copy-start.1 = (bf16[2,48,12,1024]{3,1,2,0:T(8,128)(2,1)S(1)}, bf16[2,48,12,1024]{3,1,2,0:T(8,128)(2,1)}, u32[]{:S(2)}) copy-start(bf16[2,48,12,1024]{3,1,2,0:T(8,128)(2,1)} %param.17) | copy-start | bytes 7077892
  4.0 1.0 %copy-start.2 = (bf16[512,384]{1,0:T(8,128)(2,1)S(1)}, bf16[512,384]{1,0:T(8,128)(2,1)}, u32[]{:S(2)}) copy-start(bf16[512,384]{1,0:T(8,128)(2,1)} %constant.7.clone.two_hbm) | copy-start | bytes 1179652
  5.0 1.0 %copy-start.3 = (bf16[384,512]{1,0:T(8,128)(2,1)S(1)}, bf16[384,512]{1,0:T(8,128)(2,1)}, u32[]{:S(2)}) copy-start(bf16[384,512]{1,0:T(8,128)(2,1)} %constant.6.clone.one_hbm) | copy-start | bytes 1179652
  6.0 0.9 %copy-start.4 = (f32[2,12,1024]{2,0,1:T(2,128)S(1)}, f32[2,12,1024]{2,0,1:T(2,128)}, u32[]{:S(2)}) copy-start(f32[2,12,1024]{2,0,1:T(2,128)} %param.11) | copy-start | bytes 294916
  6.9 0.9 %copy-start.5 = (f32[2,12,1024]{2,0,1:T(2,128)S(1)}, f32[2,12,1024]{2,0,1:T(2,128)}, u32[]{:S(2)}) copy-start(f32[2,12,1024]{2,0,1:T(2,128)} %param.12) | copy-start | bytes 294916
  7.7 0.8 %copy-start.6 = (bf16[128,128]{1,0:T(8,128)(2,1)S(1)}, bf16[128,128]{1,0:T(8,128)(2,1)}, u32[]{:S(2)}) copy-start(bf16[128,128]{1,0:T(8,128)(2,1)} %constant.8.clone.three_hbm) | copy-start | bytes 98308
  8.5 0.7 %copy-start.7 = (f32[32,32]{1,0:T(8,128)S(1)}, f32[32,32]{1,0:T(8,128)}, u32[]{:S(2)}) copy-start(f32[32,32]{1,0:T(8,128)} %c_hbm.1) | copy-start | bytes 12292
  9.2 0.7 %copy-start.8 = (f32[12,32]{1,0:T(8,128)S(1)}, f32[12,32]{1,0:T(8,128)}, u32[]{:S(2)}) copy-start(f32[12,32]{1,0:T(8,128)} %damp_hbm.1) | copy-start | bytes 4612
  9.9 0.7 %copy-start.9 = (f32[12,32]{1,0:T(8,128)S(1)}, f32[12,32]{1,0:T(8,128)}, u32[]{:S(2)}) copy-start(f32[12,32]{1,0:T(8,128)} %phase_hbm.1) | copy-start | bytes 4612

commit v2 on v1

--- a/solution.py
+++ b/solution.py
@@ -14,7 +14,8 @@
 HIGHEST = lax.Precision.HIGHEST
 NX = 4
 NZ = 8
-NR = 8
+NY = 4
+NH = NX * NZ
 TP = 12
 TR = 48
 OWNERS = 6
@@ -43,12 +44,13 @@
     out_ref, col_ref,
     xv, yv, cv, dampv, phasev, lesv, advv, retv, onev, twov, threev,
     sig_own, sig_all, bmat, col_acc, col_send, col_x, colz_send, col_z, col_own, col_all,
-    lmat, fpart, rs_buf, ag_buf, tot_x, tot_z, nrm_x, nrm_z, facv, stepv,
+    lmat, fpart, rs_buf, y_buf, ag_buf, tot_x, tot_z, norms, facv, stepv,
     load_sem, send_sem, recv_sem,
 ):
     h = lax.axis_index("hist")
     r = lax.axis_index("row")
     z, x = h // NX, h % NX
+    y, core = r // 2, r % 2
     dz = (z - r + NZ) % NZ
     early = z <= r
     late = z >= r
@@ -59,8 +61,14 @@
     def at_z(d):
         return {"hist": ((z + d + NZ) % NZ) * NX + x}
 
-    def at_r(d):
-        return {"row": (r + d) % NR}
+    def at_h(d):
+        return {"hist": (h + d) % NH}
+
+    def at_core():
+        return {"row": 2 * y + 1 - core}
+
+    def at_y(d):
+        return {"row": 2 * ((y + d) % NY) + core}
 
     counts = {"send": 0, "recv": 0}
     pending = []
@@ -98,12 +106,10 @@
     (c_load, x_load, y_load, damp_load, phase_load, one_load, two_load, three_load, ret_load, les_load, adv_load) = loads
 
     barrier = pltpu.get_barrier_semaphore()
-    for d in range(1, NX):
-        pl.semaphore_signal(barrier, inc=1, device_id=at_x(d), device_id_type=MESH)
-    for d in range(1, NZ):
-        pl.semaphore_signal(barrier, inc=1, device_id=at_z(d), device_id_type=MESH)
-    for d in range(1, NR):
-        pl.semaphore_signal(barrier, inc=1, device_id=at_r(d), device_id_type=MESH)
+    for d in range(1, NH):
+        pl.semaphore_signal(barrier, inc=1, device_id=at_h(d), device_id_type=MESH)
+    for device in [at_core()] + [at_y(d) for d in range(1, NY)]:
+        pl.semaphore_signal(barrier, inc=1, device_id=device, device_id_type=MESH)
 
     lane8 = lax.broadcasted_iota(jnp.int32, (8, 128), 1) // 32
 
@@ -167,21 +173,29 @@
     tot = jnp.concatenate([tot, jnp.zeros((1, 64), F32)], axis=1)
     tot_x[x] = jnp.broadcast_to(tot, (8, 128))
 
-    pl.semaphore_wait(barrier, (NX - 1) + (NZ - 1) + (NR - 1))
-
-    source = dz == 0
-    up = (dz == 1) | (dz == 2) | (dz == 3)
-    down = (dz == 7) | (dz == 6)
-    z_send, z_recv = slots("send", 4), slots("recv", 2)
-    f_send = slots("send", 4)
+    pl.semaphore_wait(barrier, (NH - 1) + 1 + (NY - 1))
+
+    source = z == r
+    z_send, z_recv = slots("send", 14), slots("recv", 2)
+    for a in range(2):
+        for d in (4, 3, 5, 2, 6, 1, 7):
+            cond = source if a == 0 else source & ((z + d) % NZ > r)
+            start(cond, sig_own.at[a], sig_all.at[a, x], z_send + 7 * a + d - 1, z_recv + a, at_z(d))
+
+    @pl.when(source)
+    def _():
+        sig_all[:, x] = sig_own[...]
+
     sx_send, sx_recv = slots("send", 6), slots("recv", 6)
+
+    def round_x(a, cond):
+        for d in range(1, NX):
+            start(
+                cond, sig_all.at[a, x], sig_all.at[a, x], sx_send + 3 * a + d - 1, sx_recv + 3 * a + d - 1, at_x(d)
+            )
+
     for a in range(2):
-        start(source, sig_own.at[a], sig_all.at[a, x], z_send + 2 * a, z_recv + a, at_z(1))
-        start(source, sig_own.at[a], sig_all.at[a, x], z_send + 2 * a + 1, z_recv + a, at_z(-1))
-
-    @pl.when(source)
-    def _():
-        sig_all[:, x] = sig_own[...]
+        round_x(a, source)
 
     tx_send, tx_recv = slots("send", 3), slots("recv", 3)
     for d in range(1, NX):
@@ -202,26 +216,6 @@
             bmat[s, pl.ds(0, 128), pl.ds(128, 128)] = b1.astype(BF16)
             bmat[s, pl.ds(128, 128), pl.ds(0, 128)] = (-b1).astype(BF16)
             bmat[s, pl.ds(128, 128), pl.ds(128, 128)] = b0.astype(BF16)
-
-    for a in range(2):
-        @pl.when(jnp.logical_not(source))
-        def _():
-            arrived(sig_own.at[a], z_recv + a)
-
-        start(up, sig_all.at[a, x], sig_all.at[a, x], f_send + 2 * a, z_recv + a, at_z(1))
-        start(down, sig_all.at[a, x], sig_all.at[a, x], f_send + 2 * a + 1, z_recv + a, at_z(-1))
-        for d in range(1, NX):
-            start(
-                None if a == 0 else late, sig_all.at[a, x], sig_all.at[a, x],
-                sx_send + 3 * a + d - 1, sx_recv + 3 * a + d - 1, at_x(d),
-            )
-
-    tz_send, tz_recv = slots("send", 7), slots("recv", 7)
-    for d in range(1, NX):
-        arrived(tot_x.at[0], tx_recv + d - 1)
-    tot_z[z] = tot_x[0] + tot_x[1] + tot_x[2] + tot_x[3]
-    for d in range(1, NZ):
-        start(None, tot_z.at[z], tot_z.at[z], tz_send + d - 1, tz_recv + d - 1, at_z(d))
 
     weight = float(NX * NZ * TP * 32) ** -0.5
     ret_load.wait()
@@ -255,6 +249,38 @@
 
     for d in range(1, NX):
         start(early, col_send.at[(x + d) % NX], col_x.at[d - 1], cx_send + d - 1, cx_recv + d - 1, at_x(d))
+
+    for a, cond in enumerate((jnp.logical_not(source), z > r)):
+        @pl.when(cond)
+        def _():
+            arrived(sig_own.at[a], z_recv + a)
+
+        round_x(a, cond)
+
+    tz_send, tz_recv = slots("send", 7), slots("recv", 7)
+    for d in range(1, NX):
+        arrived(tot_x.at[0], tx_recv + d - 1)
+    tot_z[z] = tot_x[0] + tot_x[1] + tot_x[2] + tot_x[3]
+    for d in range(1, NZ):
+        start(None, tot_z.at[z], tot_z.at[z], tz_send + d - 1, tz_recv + d - 1, at_z(d))
+
+    cz_send, cz_recv = slots("send", 7), slots("recv", 7)
+
+    @pl.when(early)
+    def _():
+        for d in range(1, NX):
+            arrived(col_x.at[d - 1], cx_recv + d - 1)
+        total = col_send[x].astype(F32)
+        for d in range(1, NX):
+            total = total + col_x[d - 1].astype(F32)
+        for j in range(OWNERS):
+            colz_send[j] = total[j * 32 : j * 32 + 32]
+
+    for d in range(1, NZ):
+        to = (z + d) % NZ
+        start(
+            early & (to < OWNERS), colz_send.at[lax.rem(to, OWNERS)], col_z.at[d - 1], cz_send + d - 1, cz_recv + d - 1, at_z(d)
+        )
 
     one_load.wait()
     two_load.wait()
@@ -280,8 +306,9 @@
 
     s_row = lax.broadcasted_iota(jnp.int32, (TR, 128), 0)
 
-    def contract(ref, masked):
-        def step(pair, carry):
+    def contract(ref, masked, half):
+        def step(index, carry):
+            pair = half * 3 + index
             cols = []
             for j in range(2):
                 t = pair * 2 + j
@@ -308,13 +335,14 @@
                         fpart[at] = total
             return carry
 
-        lax.fori_loop(0, TP // 2, step, 0)
+        lax.fori_loop(0, TP // 4, step, 0)
 
     les_load.wait()
     for d in range(1, NX):
         arrived(sig_own.at[0], sx_recv + d - 1)
     left_matrix(0)
-    contract(lesv, False)
+    contract(lesv, False, 1 - core)
+    contract(lesv, False, core)
     adv_load.wait()
 
     @pl.when(late)
@@ -322,29 +350,46 @@
         for d in range(1, NX):
             arrived(sig_own.at[1], sx_recv + 3 + d - 1)
         left_matrix(1)
-        contract(advv, True)
-
-    rs_send, rs_recv = slots("send", 7), slots("recv", 7)
-    for d in range(1, NR):
-        start(None, fpart.at[pl.ds(3 * ((r + d) % NR), 3)], rs_buf.at[d - 1], rs_send + d - 1, rs_recv + d - 1, at_r(d))
-
-    cz_send, cz_recv = slots("send", 7), slots("recv", 7)
-
-    @pl.when(early)
-    def _():
-        for d in range(1, NX):
-            arrived(col_x.at[d - 1], cx_recv + d - 1)
-        total = col_send[x].astype(F32)
-        for d in range(1, NX):
-            total = total + col_x[d - 1].astype(F32)
-        for j in range(OWNERS):
-            colz_send[j] = total[j * 32 : j * 32 + 32]
-
+        contract(advv, True, 1 - core)
+
+    rc_send, rc_recv = slots("send", 1), slots("recv", 1)
+    start(None, fpart.at[pl.ds(TP * (1 - core), TP)], rs_buf, rc_send, rc_recv, at_core())
+
+    @pl.when(late)
+    def _():
+        contract(advv, True, core)
+
+    arrived(rs_buf, rc_recv)
+    ry_send, ry_recv = slots("send", 3), slots("recv", 3)
+    half = fpart[pl.ds(TP * core, TP)] + rs_buf[...]
+    y_buf[y] = half.reshape(TP * 8, 128).astype(BF16)
+    for d in range(1, NY):
+        start(None, y_buf.at[y], y_buf.at[y], ry_send + d - 1, ry_recv + d - 1, at_y(d))
+
+    cg_send, cg_recv = slots("send", 7), slots("recv", 7)
+    owner = z < OWNERS
+
+    @pl.when(owner)
+    def _():
+        @pl.when(early)
+        def _():
+            col_own[...] = colz_send[lax.rem(z, OWNERS)]
+
+        @pl.when(jnp.logical_not(early))
+        def _():
+            col_own[...] = jnp.zeros_like(col_own)
+
+        for d in range(1, NZ):
+            @pl.when((z - d + NZ) % NZ <= r)
+            def _():
+                arrived(col_z.at[d - 1], cz_recv + d - 1)
+                col_own[...] += col_z[d - 1]
+
+        col_all[x, lax.rem(z, OWNERS)] = col_own[...].astype(BF16)
+
+    piece = col_all.at[x, lax.rem(z, OWNERS)]
     for d in range(1, NZ):
-        to = (z + d) % NZ
-        start(
-            early & (to < OWNERS), colz_send.at[lax.rem(to, OWNERS)], col_z.at[d - 1], cz_send + d - 1, cz_recv + d - 1, at_z(d)
-        )
+        start(owner, piece, piece, cg_send + d - 1, cg_recv + d - 1, at_z(d))
 
     for d in range(1, NZ):
         arrived(tot_z.at[0], tz_recv + d - 1)
@@ -366,42 +411,17 @@
     for c in range(8):
         facv[pl.ds(c, 2 * TP, stride=8), :] = spread[:, c * 128 : c * 128 + 128]
 
-    ag_send, ag_recv = slots("send", 7), slots("recv", 7)
-    own = fpart[pl.ds(3 * r, 3)]
-    for d in range(1, NR):
-        arrived(rs_buf.at[d - 1], rs_recv + d - 1)
-        own = own + rs_buf[d - 1]
-    ag_buf[pl.ds(3 * r, 3)] = own
-    for d in range(1, NR):
-        start(None, ag_buf.at[pl.ds(3 * r, 3)], ag_buf.at[pl.ds(3 * r, 3)], ag_send + d - 1, ag_recv + d - 1, at_r(d))
-
-    cg_send, cg_recv = slots("send", 7), slots("recv", 7)
-    owner = z < OWNERS
-
-    @pl.when(owner)
-    def _():
-        @pl.when(early)
-        def _():
-            col_own[...] = colz_send[lax.rem(z, OWNERS)]
-
-        @pl.when(jnp.logical_not(early))
-        def _():
-            col_own[...] = jnp.zeros_like(col_own)
-
-        for d in range(1, NZ):
-            @pl.when((z - d + NZ) % NZ <= r)
-            def _():
-                arrived(col_z.at[d - 1], cz_recv + d - 1)
-                col_own[...] += col_z[d - 1]
-
-        col_all[x, lax.rem(z, OWNERS)] = col_own[...].astype(BF16)
-
-    piece = col_all.at[x, lax.rem(z, OWNERS)]
-    for d in range(1, NZ):
-        start(owner, piece, piece, cg_send + d - 1, cg_recv + d - 1, at_z(d))
-
-    for d in range(1, NR):
-        arrived(rs_buf.at[0], ag_recv + d - 1)
+    ra_send, ra_recv = slots("send", 1), slots("recv", 1)
+    for d in range(1, NY):
+        arrived(y_buf.at[0], ry_recv + d - 1)
+    half = y_buf[0].astype(F32)
+    for j in range(1, NY):
+        half = half + y_buf[j].astype(F32)
+    ag_buf[pl.ds(TP * core, TP)] = half.reshape(TP, 8, 128)
+    piece = ag_buf.at[pl.ds(TP * core, TP)]
+    start(None, piece, piece, ra_send, ra_recv, at_core())
+
+    arrived(rs_buf, ra_recv)
     squares = jnp.zeros((8, 128), F32)
     for t in range(TP):
         fr, fi = facv[pl.ds(t * 8, 8), :], facv[pl.ds((TP + t) * 8, 8), :]
@@ -411,10 +431,10 @@
         stepv[2 * t] = step_r
         stepv[2 * t + 1] = step_i
         squares = squares + (step_r * step_r + step_i * step_i)
-    nrm_x[x] = squares
-    nx_send, nx_recv = slots("send", 3), slots("recv", 3)
-    for d in range(1, NX):
-        start(None, nrm_x.at[x], nrm_x.at[x], nx_send + d - 1, nx_recv + d - 1, at_x(d))
+    norms[h] = jnp.sum(squares, axis=0, keepdims=True)
+    n_send, n_recv = slots("send", NH - 1), slots("recv", NH - 1)
+    for d in range(1, NH):
+        start(None, norms.at[h], norms.at[h], n_send + d - 1, n_recv + d - 1, at_h(d))
 
     ca_send, ca_recv = slots("send", 3), slots("recv", 3)
     for d in range(1, NZ):
@@ -424,18 +444,10 @@
     for d in range(1, NX):
         start(None, col_all.at[x], col_all.at[x], ca_send + d - 1, ca_recv + d - 1, at_x(d))
 
-    nz_send, nz_recv = slots("send", 7), slots("recv", 7)
-    for d in range(1, NX):
-        arrived(nrm_x.at[0], nx_recv + d - 1)
-    nrm_z[z] = nrm_x[0] + nrm_x[1] + nrm_x[2] + nrm_x[3]
-    for d in range(1, NZ):
-        start(None, nrm_z.at[z], nrm_z.at[z], nz_send + d - 1, nz_recv + d - 1, at_z(d))
-    for d in range(1, NZ):
-        arrived(nrm_z.at[0], nz_recv + d - 1)
-    total = nrm_z[0]
-    for j in range(1, NZ):
-        total = total + nrm_z[j]
-    total = jnp.sum(jnp.sum(total, axis=0, keepdims=True), axis=1, keepdims=True)
+    for d in range(1, NH):
+        arrived(norms.at[0], n_recv + d - 1)
+    total = jnp.sum(norms[...], axis=0)
+    total = jnp.sum(total, axis=1, keepdims=True)
     scale = 1.0 / jnp.sqrt(total / float(2 * NX * NZ * TP * 1024) + 1e-6)
     for t in range(TP):
         out_ref[pl.ds(t * 16, 8, stride=2), :] = stepv[2 * t] * scale
@@ -443,7 +455,12 @@
 
     for d in range(1, NX):
         arrived(col_all.at[0], ca_recv + d - 1)
-    col_ref[...] = col_all[...]
+    for j in range(NX):
+        rows = col_all[j].reshape(4 * TR, 128)
+        for c in range(2):
+            for po in range(2):
+                first = (2 * c + po) * TR
+                col_ref[po, :, pl.ds((2 * j + c) * 128, 128)] = rows[first : first + TR]
 
     for cond, args in pending:
         if cond is None:
@@ -455,8 +472,8 @@
     assert counts["send"] <= SENDS and counts["recv"] <= RECVS, counts
 
 
-SENDS = 80
-RECVS = 64
+SENDS = 112
+RECVS = 96
 
 
 def shards(row_less, row_great, coupling, damping, phases, lesser_hist, advanced_hist, retarded_hist):
@@ -465,7 +482,7 @@
         return a.transpose(0, 2, 1, 3).reshape(TP * 16, 128)
 
     one, two, three = (jnp.asarray(m, BF16) for m in lane_order())
-    anywhere = pl.BlockSpec(memory_space=pl.ANY)
+    anywhere = pl.BlockSpec(memory_space=pltpu.HBM)
     vmem = pl.BlockSpec(memory_space=pltpu.VMEM)
     scratch = [
         pltpu.VMEM((TP * 16, 128), F32),
@@ -491,38 +508,40 @@
         pltpu.VMEM((NX, OWNERS, 32, 128), BF16),
         pltpu.VMEM((256, 768), BF16),
         pltpu.VMEM((2 * TP, 8, 128), F32),
-        pltpu.VMEM((NR - 1, 3, 8, 128), F32),
+        pltpu.VMEM((TP, 8, 128), F32),
+        pltpu.VMEM((NY, TP * 8, 128), BF16),
         pltpu.VMEM((2 * TP, 8, 128), F32),
         pltpu.VMEM((NX, 8, 128), F32),
         pltpu.VMEM((NZ, 8, 128), F32),
-        pltpu.VMEM((NX, 8, 128), F32),
-        pltpu.VMEM((NZ, 8, 128), F32),
+        pltpu.VMEM((NH, 1, 128), F32),
         pltpu.VMEM((2 * TP * 8, 128), F32),
         pltpu.VMEM((2 * TP, 8, 128), F32),
         pltpu.SemaphoreType.DMA((11,)),
         pltpu.SemaphoreType.DMA((SENDS,)),
         pltpu.SemaphoreType.DMA((RECVS,)),
     ]
+    operands = (
+        rows(row_less), rows(row_great), coupling, damping, phases,
+        lesser_hist.transpose(0, 2, 1, 3), advanced_hist.transpose(0, 2, 1, 3), retarded_hist.transpose(0, 2, 1, 3),
+        one, two, three,
+    )
     stepped, column = pl.pallas_call(
         body,
         out_shape=(
             jax.ShapeDtypeStruct((TP * 16, 128), F32),
-            jax.ShapeDtypeStruct((NX, OWNERS, 32, 128), BF16),
+            jax.ShapeDtypeStruct((2, TR, 1024), BF16),
         ),
         in_specs=[anywhere] * 11,
         out_specs=(vmem, vmem),
         scratch_shapes=scratch,
         compiler_params=pltpu.CompilerParams(
-            collective_id=0, has_side_effects=True, vmem_limit_bytes=48 * 1024 * 1024
+            collective_id=0, has_side_effects=True, vmem_limit_bytes=24 * 1024 * 1024
         ),
         name="kadanoff_baym_step",
     )(
-        rows(row_less), rows(row_great), coupling, damping, phases,
-        lesser_hist.transpose(0, 2, 1, 3), advanced_hist.transpose(0, 2, 1, 3), retarded_hist.transpose(0, 2, 1, 3),
-        one, two, three,
+        *(pltpu.with_memory_space_constraint(a, pltpu.HBM) for a in operands)
     )
     stepped = stepped.reshape(TP, 8, 2, 128).transpose(2, 0, 1, 3).reshape(2, TP, 1024)
-    column = column.reshape(NX, 2, 2, TR, 128).transpose(2, 3, 0, 1, 4).reshape(2, TR, 1024)
     return stepped, column.astype(F32)
 
 

time: 61.8 us -> 41.2 us (0.67)
  local copies, waits for them, and re-layouts: 12 us -> 0.64 us
  Pallas kernels: 48.5 us -> 39 us
  other arithmetic: 0.03 us -> 0.78 us
    unnamed x21 -> x1, local copies, waits for them, and re-layouts: 10.6 us -> 0.64 us
    pallas_call x1, Pallas kernels: 48.5 us -> 39 us  [shards(): pl.pallas_call(body, out_shape=(jax.ShapeDtypeStruct((TP * 16, 128), F32)...]
    convert_element_type x2 -> x0, local copies, waits for them, and re-layouts: 1.37 us -> none  [shards(): return (stepped, column.astype(F32))]
    convert_element_type x1, other arithmetic: 0.03 us -> 0.78 us  [shards(): return (stepped, column.astype(F32))]
where the time goes in v2:
time: 41.2 us; the launch traced here: 41.1 us
  Pallas kernels  39 us (95%)
  other arithmetic  0.78 us (2%)
  local copies, waits for them, and re-layouts  0.64 us (2%)
  between operations  0.64 us (2%)
    pallas_call x1, Pallas kernels, shards(): pl.pallas_call(body, out_shape=(jax.ShapeDtypeStruct((TP * 16, 128), F32)...  39 us

profile of v2, /device:TPU:1, one launch (start us, length us, event | category | flops | bytes accessed | tf_op | source)
XLA Modules:
  0.0 41.1 jit_solution(7208132346079200212)
XLA Ops:
  0.6 39.0 %kadanoff_baym_step.1 = (f32[192,128]{1,0:T(8,128)S(1)}, bf16[2,48,1024]{2,1,0:T(8,128)(2,1)S(1)}) custom-call(f32[192,128]{1,0:T(8,128)} %bitcast.26, f32[192,128]{1,0:T(8,128)} %bitcast.27, f32[32,32]{1,0:T(8,128)} %c_hbm.1, f32[12,32]{1,0:T(8,128)} %damp_hbm.1, f32[12,32]{1,0:T(8,128)} %phase_hbm.1, bf16[2,12,48,1024]{3,2,1,0:T(8,128)(2,1)} %bitcast.23, ...), custom_call_target="tpu_custom_call" | custom-call | tf_op jit(solution)/shard_map/kadanoff_baym_step/pallas_call | solution.py:528
  39.6 0.8 %convert_element_type.3 = f32[2,48,1024]{2,1,0:T(8,128)} convert(bf16[2,48,1024]{2,1,0:T(8,128)(2,1)S(1)} %get-tuple-element.5) | non-fusion elementwise | flops 98304 | bytes 589824 | tf_op jit(solution)/shard_map/convert_element_type | solution.py:545
  40.4 0.6 %copy.17 = f32[2,12,1024]{2,0,1:T(2,128)} copy(f32[2,12,1024]{2,0,1:T(2,128)S(1)} %bitcast.22) | data formatting | bytes 196608

commit v3 on v2

--- a/solution.py
+++ b/solution.py
@@ -14,8 +14,21 @@
 HIGHEST = lax.Precision.HIGHEST
 NX = 4
 NZ = 8
-NY = 4
+NR = 8
 NH = NX * NZ
+
+
+def ring(n, d):
+    return min(d, n - d)
+
+
+SPREAD = {0: 4, 1: 3, 2: 5, 3: 2, 4: 7, 5: 0, 6: 6, 7: 1}
+FAR_X = sorted(range(1, NX), key=lambda d: -ring(NX, d))
+FAR_Z = sorted(range(1, NZ), key=lambda d: -ring(NZ, d))
+FAR_R = sorted(range(1, NR), key=lambda d: -ring(NR, d))
+FAR_H = sorted(
+    ((dz, dx) for dz in range(NZ) for dx in range(NX) if dz or dx), key=lambda d: -ring(NZ, d[0]) - ring(NX, d[1])
+)
 TP = 12
 TR = 48
 OWNERS = 6
@@ -44,7 +57,7 @@
     out_ref, col_ref,
     xv, yv, cv, dampv, phasev, lesv, advv, retv, onev, twov, threev,
     sig_own, sig_all, bmat, col_acc, col_send, col_x, colz_send, col_z, col_own, col_all,
-    lmat, fpart, rs_buf, y_buf, ag_buf, tot_x, tot_z, norms, facv, stepv,
+    lmat, fpart, rs_buf, y_buf, tot_x, tot_z, norms, facv, stepv,
     load_sem, send_sem, recv_sem,
 ):
     h = lax.axis_index("hist")
@@ -53,6 +66,8 @@
     y, core = r // 2, r % 2
     dz = (z - r + NZ) % NZ
     early = z <= r
+    source = z == r
+    place = (y - z // 2 + 4) % 4 * 2 + (core + z) % 2
     late = z >= r
 
     def at_x(d):
@@ -62,13 +77,13 @@
         return {"hist": ((z + d + NZ) % NZ) * NX + x}
 
     def at_h(d):
-        return {"hist": (h + d) % NH}
+        return {"hist": (z + d[0]) % NZ * NX + (x + d[1]) % NX}
 
     def at_core():
         return {"row": 2 * y + 1 - core}
 
-    def at_y(d):
-        return {"row": 2 * ((y + d) % NY) + core}
+    def at_r(d):
+        return {"row": (r + d) % NR}
 
     counts = {"send": 0, "recv": 0}
     pending = []
@@ -106,10 +121,17 @@
     (c_load, x_load, y_load, damp_load, phase_load, one_load, two_load, three_load, ret_load, les_load, adv_load) = loads
 
     barrier = pltpu.get_barrier_semaphore()
-    for d in range(1, NH):
-        pl.semaphore_signal(barrier, inc=1, device_id=at_h(d), device_id_type=MESH)
-    for device in [at_core()] + [at_y(d) for d in range(1, NY)]:
+    for d in range(1, NX):
+        pl.semaphore_signal(barrier, inc=1, device_id=at_x(d), device_id_type=MESH)
+    for d in range(1, NZ):
+        pl.semaphore_signal(barrier, inc=1, device_id=at_z(d), device_id_type=MESH)
+    for device in [at_r(d) for d in range(1, NR)]:
         pl.semaphore_signal(barrier, inc=1, device_id=device, device_id_type=MESH)
+    for k, d in SPREAD.items():
+        @pl.when((z - r + NZ) % NZ == d)
+        def _():
+            holder = (r // 2 + k // 2) % 4 * 2 + (r + k) % 2
+            pl.semaphore_signal(barrier, inc=1, device_id={"hist": r * NX + x, "row": holder}, device_id_type=MESH)
 
     lane8 = lax.broadcasted_iota(jnp.int32, (8, 128), 1) // 32
 
@@ -173,14 +195,17 @@
     tot = jnp.concatenate([tot, jnp.zeros((1, 64), F32)], axis=1)
     tot_x[x] = jnp.broadcast_to(tot, (8, 128))
 
-    pl.semaphore_wait(barrier, (NH - 1) + 1 + (NY - 1))
-
-    source = z == r
-    z_send, z_recv = slots("send", 14), slots("recv", 2)
+    pl.semaphore_wait(barrier, (NX - 1) + (NZ - 1) + (NR - 1) + 1)
+
+    z_send, z_recv = slots("send", 2), slots("recv", 2)
     for a in range(2):
-        for d in (4, 3, 5, 2, 6, 1, 7):
-            cond = source if a == 0 else source & ((z + d) % NZ > r)
-            start(cond, sig_own.at[a], sig_all.at[a, x], z_send + 7 * a + d - 1, z_recv + a, at_z(d))
+        for k, d in SPREAD.items():
+            if d == 0:
+                continue
+            start(
+                (place == k) if a == 0 else (place == k) & ((z + d) % NZ > z),
+                sig_own.at[a], sig_all.at[a, x], z_send + a, z_recv + a, {"hist": (z + d) % NZ * NX + x, "row": z},
+            )
 
     @pl.when(source)
     def _():
@@ -189,7 +214,7 @@
     sx_send, sx_recv = slots("send", 6), slots("recv", 6)
 
     def round_x(a, cond):
-        for d in range(1, NX):
+        for d in FAR_X:
             start(
                 cond, sig_all.at[a, x], sig_all.at[a, x], sx_send + 3 * a + d - 1, sx_recv + 3 * a + d - 1, at_x(d)
             )
@@ -198,7 +223,7 @@
         round_x(a, source)
 
     tx_send, tx_recv = slots("send", 3), slots("recv", 3)
-    for d in range(1, NX):
+    for d in FAR_X:
         start(None, tot_x.at[x], tot_x.at[x], tx_send + d - 1, tx_recv + d - 1, at_x(d))
 
     @pl.when(early)
@@ -212,10 +237,10 @@
 
         for s in range(TP):
             b0, b1 = square_of(0, s), square_of(1, s)
-            bmat[s, pl.ds(0, 128), pl.ds(0, 128)] = b0.astype(BF16)
-            bmat[s, pl.ds(0, 128), pl.ds(128, 128)] = b1.astype(BF16)
-            bmat[s, pl.ds(128, 128), pl.ds(0, 128)] = (-b1).astype(BF16)
-            bmat[s, pl.ds(128, 128), pl.ds(128, 128)] = b0.astype(BF16)
+            bmat[s // 4, pl.ds(0, 128), pl.ds(s % 4 * 256, 128)] = b0.astype(BF16)
+            bmat[s // 4, pl.ds(0, 128), pl.ds(s % 4 * 256 + 128, 128)] = b1.astype(BF16)
+            bmat[s // 4, pl.ds(128, 128), pl.ds(s % 4 * 256, 128)] = (-b1).astype(BF16)
+            bmat[s // 4, pl.ds(128, 128), pl.ds(s % 4 * 256 + 128, 128)] = b0.astype(BF16)
 
     weight = float(NX * NZ * TP * 32) ** -0.5
     ret_load.wait()
@@ -227,27 +252,29 @@
         t_row = lax.broadcasted_iota(jnp.int32, (TR, 128), 0)
         col_acc[...] = jnp.zeros_like(col_acc)
 
-        def step(s, carry):
-            keep = t_row >= h * TP + s - r * TR
-            rows = [
-                jnp.concatenate(
-                    [jnp.where(keep, retv[p, s, :, pl.ds(c * 128, 128)], jnp.zeros((), BF16)) for p in range(2)], axis=1
-                )
-                for c in range(8)
-            ]
+        def step(group, carry):
+            rows = []
+            for c in range(8):
+                lanes = []
+                for k in range(4):
+                    at = group * 4 + k
+                    keep = t_row >= h * TP + at - r * TR
+                    for p in range(2):
+                        lanes.append(jnp.where(keep, retv[p, at, :, pl.ds(c * 128, 128)], jnp.zeros((), BF16)))
+                rows.append(jnp.concatenate(lanes, axis=1))
             col_acc[...] += lax.dot_general(
-                jnp.concatenate(rows, axis=0), bmat[s], LANES_TO_LANES, preferred_element_type=F32
+                jnp.concatenate(rows, axis=0), bmat[group], LANES_TO_LANES, preferred_element_type=F32
             )
             return carry
 
-        lax.fori_loop(0, TP, step, 0)
+        lax.fori_loop(0, TP // 4, step, 0)
         for c in range(8):
             for po in range(2):
                 value = (col_acc[pl.ds(c * TR, TR), pl.ds(po * 128, 128)] * -weight).astype(BF16)
                 value = jnp.dot(value, threev[...], preferred_element_type=F32)
                 col_send[c // 2, pl.ds(((c % 2) * 2 + po) * TR, TR), :] = value.astype(BF16)
 
-    for d in range(1, NX):
+    for d in FAR_X:
         start(early, col_send.at[(x + d) % NX], col_x.at[d - 1], cx_send + d - 1, cx_recv + d - 1, at_x(d))
 
     for a, cond in enumerate((jnp.logical_not(source), z > r)):
@@ -261,7 +288,7 @@
     for d in range(1, NX):
         arrived(tot_x.at[0], tx_recv + d - 1)
     tot_z[z] = tot_x[0] + tot_x[1] + tot_x[2] + tot_x[3]
-    for d in range(1, NZ):
+    for d in FAR_Z:
         start(None, tot_z.at[z], tot_z.at[z], tz_send + d - 1, tz_recv + d - 1, at_z(d))
 
     cz_send, cz_recv = slots("send", 7), slots("recv", 7)
@@ -276,7 +303,7 @@
         for j in range(OWNERS):
             colz_send[j] = total[j * 32 : j * 32 + 32]
 
-    for d in range(1, NZ):
+    for d in FAR_Z:
         to = (z + d) % NZ
         start(
             early & (to < OWNERS), colz_send.at[lax.rem(to, OWNERS)], col_z.at[d - 1], cz_send + d - 1, cz_recv + d - 1, at_z(d)
@@ -335,7 +362,7 @@
                         fpart[at] = total
             return carry
 
-        lax.fori_loop(0, TP // 4, step, 0)
+        lax.fori_loop(0, TP // 4, step, 0, unroll=True)
 
     les_load.wait()
     for d in range(1, NX):
@@ -343,6 +370,31 @@
     left_matrix(0)
     contract(lesv, False, 1 - core)
     contract(lesv, False, core)
+    cg_send, cg_recv = slots("send", 7), slots("recv", 7)
+    owner = z < OWNERS
+
+    @pl.when(owner)
+    def _():
+        @pl.when(early)
+        def _():
+            col_own[...] = colz_send[lax.rem(z, OWNERS)]
+
+        @pl.when(jnp.logical_not(early))
+        def _():
+            col_own[...] = jnp.zeros_like(col_own)
+
+        for d in range(1, NZ):
+            @pl.when((z - d + NZ) % NZ <= r)
+            def _():
+                arrived(col_z.at[d - 1], cz_recv + d - 1)
+                col_own[...] += col_z[d - 1]
+
+        col_all[x, lax.rem(z, OWNERS)] = col_own[...].astype(BF16)
+
+    piece = col_all.at[x, lax.rem(z, OWNERS)]
+    for d in FAR_Z:
+        start(owner, piece, piece, cg_send + d - 1, cg_recv + d - 1, at_z(d))
+
     adv_load.wait()
 
     @pl.when(late)
@@ -360,36 +412,11 @@
         contract(advv, True, core)
 
     arrived(rs_buf, rc_recv)
-    ry_send, ry_recv = slots("send", 3), slots("recv", 3)
+    ry_send, ry_recv = slots("send", 7), slots("recv", 7)
     half = fpart[pl.ds(TP * core, TP)] + rs_buf[...]
-    y_buf[y] = half.reshape(TP * 8, 128).astype(BF16)
-    for d in range(1, NY):
-        start(None, y_buf.at[y], y_buf.at[y], ry_send + d - 1, ry_recv + d - 1, at_y(d))
-
-    cg_send, cg_recv = slots("send", 7), slots("recv", 7)
-    owner = z < OWNERS
-
-    @pl.when(owner)
-    def _():
-        @pl.when(early)
-        def _():
-            col_own[...] = colz_send[lax.rem(z, OWNERS)]
-
-        @pl.when(jnp.logical_not(early))
-        def _():
-            col_own[...] = jnp.zeros_like(col_own)
-
-        for d in range(1, NZ):
-            @pl.when((z - d + NZ) % NZ <= r)
-            def _():
-                arrived(col_z.at[d - 1], cz_recv + d - 1)
-                col_own[...] += col_z[d - 1]
-
-        col_all[x, lax.rem(z, OWNERS)] = col_own[...].astype(BF16)
-
-    piece = col_all.at[x, lax.rem(z, OWNERS)]
-    for d in range(1, NZ):
-        start(owner, piece, piece, cg_send + d - 1, cg_recv + d - 1, at_z(d))
+    y_buf[r] = half.reshape(TP * 8, 128).astype(BF16)
+    for d in FAR_R:
+        start(None, y_buf.at[r], y_buf.at[r], ry_send + d - 1, ry_recv + d - 1, at_r(d))
 
     for d in range(1, NZ):
         arrived(tot_z.at[0], tz_recv + d - 1)
@@ -411,41 +438,39 @@
     for c in range(8):
         facv[pl.ds(c, 2 * TP, stride=8), :] = spread[:, c * 128 : c * 128 + 128]
 
-    ra_send, ra_recv = slots("send", 1), slots("recv", 1)
-    for d in range(1, NY):
+    ca_send, ca_recv = slots("send", 3), slots("recv", 3)
+    for d in range(1, NZ):
+        @pl.when((z - d + NZ) % NZ < OWNERS)
+        def _():
+            arrived(col_all.at[0, 0], cg_recv + d - 1)
+    for d in FAR_X:
+        start(None, col_all.at[x], col_all.at[x], ca_send + d - 1, ca_recv + d - 1, at_x(d))
+
+    for d in range(1, NR):
         arrived(y_buf.at[0], ry_recv + d - 1)
-    half = y_buf[0].astype(F32)
-    for j in range(1, NY):
-        half = half + y_buf[j].astype(F32)
-    ag_buf[pl.ds(TP * core, TP)] = half.reshape(TP, 8, 128)
-    piece = ag_buf.at[pl.ds(TP * core, TP)]
-    start(None, piece, piece, ra_send, ra_recv, at_core())
-
-    arrived(rs_buf, ra_recv)
+    halves = []
+    for k in range(2):
+        half = y_buf[k].astype(F32)
+        for j in range(k + 2, NR, 2):
+            half = half + y_buf[j].astype(F32)
+        halves.append(half)
+
     squares = jnp.zeros((8, 128), F32)
     for t in range(TP):
         fr, fi = facv[pl.ds(t * 8, 8), :], facv[pl.ds((TP + t) * 8, 8), :]
-        ar = xv[pl.ds(t * 16, 8, stride=2), :] + ag_buf[2 * t]
-        ai = xv[pl.ds(t * 16 + 1, 8, stride=2), :] + ag_buf[2 * t + 1]
+        ar = xv[pl.ds(t * 16, 8, stride=2), :] + halves[t // 6][t % 6 * 16 : t % 6 * 16 + 8]
+        ai = xv[pl.ds(t * 16 + 1, 8, stride=2), :] + halves[t // 6][t % 6 * 16 + 8 : t % 6 * 16 + 16]
         step_r, step_i = fr * ar - fi * ai, fr * ai + fi * ar
         stepv[2 * t] = step_r
         stepv[2 * t + 1] = step_i
         squares = squares + (step_r * step_r + step_i * step_i)
     norms[h] = jnp.sum(squares, axis=0, keepdims=True)
     n_send, n_recv = slots("send", NH - 1), slots("recv", NH - 1)
-    for d in range(1, NH):
-        start(None, norms.at[h], norms.at[h], n_send + d - 1, n_recv + d - 1, at_h(d))
-
-    ca_send, ca_recv = slots("send", 3), slots("recv", 3)
-    for d in range(1, NZ):
-        @pl.when((z - d + NZ) % NZ < OWNERS)
-        def _():
-            arrived(col_all.at[0, 0], cg_recv + d - 1)
-    for d in range(1, NX):
-        start(None, col_all.at[x], col_all.at[x], ca_send + d - 1, ca_recv + d - 1, at_x(d))
-
-    for d in range(1, NH):
-        arrived(norms.at[0], n_recv + d - 1)
+    for k, d in enumerate(FAR_H):
+        start(None, norms.at[h], norms.at[h], n_send + k, n_recv + k, at_h(d))
+
+    for k in range(NH - 1):
+        arrived(norms.at[0], n_recv + k)
     total = jnp.sum(norms[...], axis=0)
     total = jnp.sum(total, axis=1, keepdims=True)
     scale = 1.0 / jnp.sqrt(total / float(2 * NX * NZ * TP * 1024) + 1e-6)
@@ -470,6 +495,19 @@
             def _():
                 copy(*args).wait_send()
     assert counts["send"] <= SENDS and counts["recv"] <= RECVS, counts
+
+
+def finish(step_ref, col_ref, step_out, col_out, wide, sems):
+    step = pltpu.make_async_copy(step_ref, step_out, sems.at[0])
+    step.start()
+    copies = []
+    for p in range(2):
+        wide[p] = col_ref[p].astype(F32)
+        copies.append(pltpu.make_async_copy(wide.at[p], col_out.at[p], sems.at[1 + p]))
+        copies[p].start()
+    for copy in copies:
+        copy.wait()
+    step.wait()
 
 
 SENDS = 112
@@ -498,7 +536,7 @@
         pltpu.VMEM((128, 128), BF16),
         pltpu.VMEM((2, 64, TP * 32), BF16),
         pltpu.VMEM((2, NX, 64, TP * 32), BF16),
-        pltpu.VMEM((TP, 256, 256), BF16),
+        pltpu.VMEM((TP // 4, 256, 1024), BF16),
         pltpu.VMEM((8 * TR, 256), F32),
         pltpu.VMEM((NX, 4 * TR, 128), BF16),
         pltpu.VMEM((NX - 1, 4 * TR, 128), BF16),
@@ -509,8 +547,7 @@
         pltpu.VMEM((256, 768), BF16),
         pltpu.VMEM((2 * TP, 8, 128), F32),
         pltpu.VMEM((TP, 8, 128), F32),
-        pltpu.VMEM((NY, TP * 8, 128), BF16),
-        pltpu.VMEM((2 * TP, 8, 128), F32),
+        pltpu.VMEM((NR, TP * 8, 128), BF16),
         pltpu.VMEM((NX, 8, 128), F32),
         pltpu.VMEM((NZ, 8, 128), F32),
         pltpu.VMEM((NH, 1, 128), F32),
@@ -541,8 +578,16 @@
     )(
         *(pltpu.with_memory_space_constraint(a, pltpu.HBM) for a in operands)
     )
-    stepped = stepped.reshape(TP, 8, 2, 128).transpose(2, 0, 1, 3).reshape(2, TP, 1024)
-    return stepped, column.astype(F32)
+    stepped, column = pl.pallas_call(
+        finish,
+        out_shape=(jax.ShapeDtypeStruct((TP * 16, 128), F32), jax.ShapeDtypeStruct((2, TR, 1024), F32)),
+        in_specs=[vmem, vmem],
+        out_specs=(pl.BlockSpec(memory_space=pltpu.HBM),) * 2,
+        scratch_shapes=[pltpu.VMEM((2, TR, 1024), F32), pltpu.SemaphoreType.DMA((3,))],
+        compiler_params=pltpu.CompilerParams(vmem_limit_bytes=4 * 1024 * 1024),
+        name="finish",
+    )(stepped, column)
+    return stepped.reshape(TP, 8, 2, 128).transpose(2, 0, 1, 3).reshape(2, TP, 1024), column
 
 
 def solution(mesh):

time: 41.2 us -> 38.1 us (0.925)
  Pallas kernels: 39 us -> 37.3 us
  other arithmetic: 0.78 us -> 0 us
  local copies, waits for them, and re-layouts: 0.64 us -> 0 us
    pallas_call x1, Pallas kernels: 39 us -> 36.5 us  [shards(): pl.pallas_call(body, out_shape=(jax.ShapeDtypeStruct((TP * 16, 128), F32)...]
    pallas_call x0 -> x1, Pallas kernels: none -> 0.8 us  [shards(): pl.pallas_call(finish, out_shape=(jax.ShapeDtypeStruct((TP * 16, 128), F3...]
    convert_element_type x1 -> x0, other arithmetic: 0.78 us -> none  [shards(): return (stepped, column.astype(F32))]
    unnamed x1 -> x0, local copies, waits for them, and re-layouts: 0.64 us -> none
where the time goes in v3:
time: 38.1 us; the launch traced here: 37.9 us
  Pallas kernels  37.3 us (98%)
  between operations  0.64 us (2%)
    pallas_call x1, Pallas kernels, shards(): pl.pallas_call(body, out_shape=(jax.ShapeDtypeStruct((TP * 16, 128), F32)...  36.5 us
    pallas_call x1, Pallas kernels, shards(): pl.pallas_call(finish, out_shape=(jax.ShapeDtypeStruct((TP * 16, 128), F3...  0.8 us

profile of v3, /device:TPU:1, one launch (start us, length us, event | category | flops | bytes accessed | tf_op | source)
XLA Modules:
  0.0 37.9 jit_solution(3429886866044362246)
XLA Ops:
  0.6 36.5 %kadanoff_baym_step.1 = (f32[192,128]{1,0:T(8,128)S(1)}, bf16[2,48,1024]{2,1,0:T(8,128)(2,1)S(1)}) custom-call(f32[192,128]{1,0:T(8,128)} %bitcast.25, f32[192,128]{1,0:T(8,128)} %bitcast.26, f32[32,32]{1,0:T(8,128)} %c_hbm.1, f32[12,32]{1,0:T(8,128)} %damp_hbm.1, f32[12,32]{1,0:T(8,128)} %phase_hbm.1, bf16[2,12,48,1024]{3,2,1,0:T(8,128)(2,1)} %bitcast.22, ...), custom_call_target="tpu_custom_call" | custom-call | tf_op jit(solution)/shard_map/kadanoff_baym_step/pallas_call | solution.py:565
  37.1 0.8 %finish.1 = (f32[192,128]{1,0:T(8,128)}, f32[2,48,1024]{2,1,0:T(8,128)}) custom-call(f32[192,128]{1,0:T(8,128)S(1)} %get-tuple-element.6.step_ref, bf16[2,48,1024]{2,1,0:T(8,128)(2,1)S(1)} %get-tuple-element.7.col_ref), custom_call_target="tpu_custom_call" | custom-call | tf_op jit(solution)/shard_map/finish/pallas_call | solution.py:581

commit v4 on v3

--- a/solution.py
+++ b/solution.py
@@ -22,7 +22,7 @@
     return min(d, n - d)
 
 
-SPREAD = {0: 4, 1: 3, 2: 5, 3: 2, 4: 7, 5: 0, 6: 6, 7: 1}
+SPREAD = {0: 4, 1: 5, 2: 3, 3: 6, 4: 1, 5: 0, 6: 2, 7: 7}
 FAR_X = sorted(range(1, NX), key=lambda d: -ring(NX, d))
 FAR_Z = sorted(range(1, NZ), key=lambda d: -ring(NZ, d))
 FAR_R = sorted(range(1, NR), key=lambda d: -ring(NR, d))
@@ -110,6 +110,16 @@
 
     def arrived(ref, recv):
         copy(ref, ref, 0, recv, at_x(1)).wait_recv()
+
+    def drain():
+        for cond, args in pending:
+            if cond is None:
+                copy(*args).wait_send()
+            else:
+                @pl.when(cond)
+                def _():
+                    copy(*args).wait_send()
+        pending.clear()
 
     loads = []
     for src, dst in (
@@ -188,39 +198,43 @@
                 )
                 sig_own[a, pl.ds(p * 32, 32), pl.ds(m * 128, 128)] = block.astype(BF16)
 
+    pl.semaphore_wait(barrier, (NX - 1) + (NZ - 1) + (NR - 1) + 1)
+
+    z_send, z_recv = slots("send", 4), slots("recv", 4)
+    for a in range(2):
+        for half in range(2):
+            rows = pl.ds(32 * half, 32)
+            for k, d in SPREAD.items():
+                if d == 0:
+                    continue
+                start(
+                    (place == k) if a == 0 else (place == k) & ((z + d) % NZ > z),
+                    sig_own.at[a, rows], sig_all.at[a, x, rows], z_send + 2 * a + half, z_recv + 2 * a + half,
+                    {"hist": (z + d) % NZ * NX + x, "row": z},
+                )
+
+    @pl.when(source)
+    def _():
+        sig_all[:, x] = sig_own[...]
+
+    sx_send, sx_recv = slots("send", 12), slots("recv", 12)
+
+    def round_x(a, half, cond):
+        block = sig_all.at[a, x, pl.ds(32 * half, 32)]
+        for d in FAR_X:
+            at = 6 * a + 3 * half + d - 1
+            start(cond, block, block, sx_send + at, sx_recv + at, at_x(d))
+
+    for a in range(2):
+        for half in range(2):
+            round_x(a, half, source)
+
     damp_load.wait()
     phase_load.wait()
     logs = jnp.concatenate([jnp.log(dampv[...]), phasev[...]], axis=1)
     tot = jnp.sum(logs, axis=0, keepdims=True)
     tot = jnp.concatenate([tot, jnp.zeros((1, 64), F32)], axis=1)
     tot_x[x] = jnp.broadcast_to(tot, (8, 128))
-
-    pl.semaphore_wait(barrier, (NX - 1) + (NZ - 1) + (NR - 1) + 1)
-
-    z_send, z_recv = slots("send", 2), slots("recv", 2)
-    for a in range(2):
-        for k, d in SPREAD.items():
-            if d == 0:
-                continue
-            start(
-                (place == k) if a == 0 else (place == k) & ((z + d) % NZ > z),
-                sig_own.at[a], sig_all.at[a, x], z_send + a, z_recv + a, {"hist": (z + d) % NZ * NX + x, "row": z},
-            )
-
-    @pl.when(source)
-    def _():
-        sig_all[:, x] = sig_own[...]
-
-    sx_send, sx_recv = slots("send", 6), slots("recv", 6)
-
-    def round_x(a, cond):
-        for d in FAR_X:
-            start(
-                cond, sig_all.at[a, x], sig_all.at[a, x], sx_send + 3 * a + d - 1, sx_recv + 3 * a + d - 1, at_x(d)
-            )
-
-    for a in range(2):
-        round_x(a, source)
 
     tx_send, tx_recv = slots("send", 3), slots("recv", 3)
     for d in FAR_X:
@@ -278,11 +292,12 @@
         start(early, col_send.at[(x + d) % NX], col_x.at[d - 1], cx_send + d - 1, cx_recv + d - 1, at_x(d))
 
     for a, cond in enumerate((jnp.logical_not(source), z > r)):
-        @pl.when(cond)
-        def _():
-            arrived(sig_own.at[a], z_recv + a)
-
-        round_x(a, cond)
+        for half in range(2):
+            @pl.when(cond)
+            def _():
+                arrived(sig_own.at[a, pl.ds(0, 32)], z_recv + 2 * a + half)
+
+            round_x(a, half, cond)
 
     tz_send, tz_recv = slots("send", 7), slots("recv", 7)
     for d in range(1, NX):
@@ -366,41 +381,18 @@
 
     les_load.wait()
     for d in range(1, NX):
-        arrived(sig_own.at[0], sx_recv + d - 1)
+        for half in range(2):
+            arrived(sig_own.at[0, pl.ds(0, 32)], sx_recv + 3 * half + d - 1)
     left_matrix(0)
     contract(lesv, False, 1 - core)
     contract(lesv, False, core)
-    cg_send, cg_recv = slots("send", 7), slots("recv", 7)
-    owner = z < OWNERS
-
-    @pl.when(owner)
-    def _():
-        @pl.when(early)
-        def _():
-            col_own[...] = colz_send[lax.rem(z, OWNERS)]
-
-        @pl.when(jnp.logical_not(early))
-        def _():
-            col_own[...] = jnp.zeros_like(col_own)
-
-        for d in range(1, NZ):
-            @pl.when((z - d + NZ) % NZ <= r)
-            def _():
-                arrived(col_z.at[d - 1], cz_recv + d - 1)
-                col_own[...] += col_z[d - 1]
-
-        col_all[x, lax.rem(z, OWNERS)] = col_own[...].astype(BF16)
-
-    piece = col_all.at[x, lax.rem(z, OWNERS)]
-    for d in FAR_Z:
-        start(owner, piece, piece, cg_send + d - 1, cg_recv + d - 1, at_z(d))
-
     adv_load.wait()
 
     @pl.when(late)
     def _():
         for d in range(1, NX):
-            arrived(sig_own.at[1], sx_recv + 3 + d - 1)
+            for half in range(2):
+                arrived(sig_own.at[1, pl.ds(0, 32)], sx_recv + 6 + 3 * half + d - 1)
         left_matrix(1)
         contract(advv, True, 1 - core)
 
@@ -417,6 +409,31 @@
     y_buf[r] = half.reshape(TP * 8, 128).astype(BF16)
     for d in FAR_R:
         start(None, y_buf.at[r], y_buf.at[r], ry_send + d - 1, ry_recv + d - 1, at_r(d))
+
+    cg_send, cg_recv = slots("send", 7), slots("recv", 7)
+    owner = z < OWNERS
+
+    @pl.when(owner)
+    def _():
+        @pl.when(early)
+        def _():
+            col_own[...] = colz_send[lax.rem(z, OWNERS)]
+
+        @pl.when(jnp.logical_not(early))
+        def _():
+            col_own[...] = jnp.zeros_like(col_own)
+
+        for d in range(1, NZ):
+            @pl.when((z - d + NZ) % NZ <= r)
+            def _():
+                arrived(col_z.at[d - 1], cz_recv + d - 1)
+                col_own[...] += col_z[d - 1]
+
+        col_all[x, lax.rem(z, OWNERS)] = col_own[...].astype(BF16)
+
+    piece = col_all.at[x, lax.rem(z, OWNERS)]
+    for d in FAR_Z:
+        start(owner, piece, piece, cg_send + d - 1, cg_recv + d - 1, at_z(d))
 
     for d in range(1, NZ):
         arrived(tot_z.at[0], tz_recv + d - 1)
@@ -438,14 +455,6 @@
     for c in range(8):
         facv[pl.ds(c, 2 * TP, stride=8), :] = spread[:, c * 128 : c * 128 + 128]
 
-    ca_send, ca_recv = slots("send", 3), slots("recv", 3)
-    for d in range(1, NZ):
-        @pl.when((z - d + NZ) % NZ < OWNERS)
-        def _():
-            arrived(col_all.at[0, 0], cg_recv + d - 1)
-    for d in FAR_X:
-        start(None, col_all.at[x], col_all.at[x], ca_send + d - 1, ca_recv + d - 1, at_x(d))
-
     for d in range(1, NR):
         arrived(y_buf.at[0], ry_recv + d - 1)
     halves = []
@@ -465,18 +474,17 @@
         stepv[2 * t + 1] = step_i
         squares = squares + (step_r * step_r + step_i * step_i)
     norms[h] = jnp.sum(squares, axis=0, keepdims=True)
-    n_send, n_recv = slots("send", NH - 1), slots("recv", NH - 1)
-    for k, d in enumerate(FAR_H):
-        start(None, norms.at[h], norms.at[h], n_send + k, n_recv + k, at_h(d))
-
-    for k in range(NH - 1):
-        arrived(norms.at[0], n_recv + k)
-    total = jnp.sum(norms[...], axis=0)
-    total = jnp.sum(total, axis=1, keepdims=True)
-    scale = 1.0 / jnp.sqrt(total / float(2 * NX * NZ * TP * 1024) + 1e-6)
-    for t in range(TP):
-        out_ref[pl.ds(t * 16, 8, stride=2), :] = stepv[2 * t] * scale
-        out_ref[pl.ds(t * 16 + 1, 8, stride=2), :] = stepv[2 * t + 1] * scale
+    n_send, n_recv = slots("send", 1), slots("recv", 1)
+    for d in FAR_H:
+        copy(norms.at[h], norms.at[h], n_send, n_recv, at_h(d)).start()
+
+    ca_send, ca_recv = slots("send", 3), slots("recv", 3)
+    for d in range(1, NZ):
+        @pl.when((z - d + NZ) % NZ < OWNERS)
+        def _():
+            arrived(col_all.at[0, 0], cg_recv + d - 1)
+    for d in FAR_X:
+        start(None, col_all.at[x], col_all.at[x], ca_send + d - 1, ca_recv + d - 1, at_x(d))
 
     for d in range(1, NX):
         arrived(col_all.at[0], ca_recv + d - 1)
@@ -486,14 +494,17 @@
             for po in range(2):
                 first = (2 * c + po) * TR
                 col_ref[po, :, pl.ds((2 * j + c) * 128, 128)] = rows[first : first + TR]
-
-    for cond, args in pending:
-        if cond is None:
-            copy(*args).wait_send()
-        else:
-            @pl.when(cond)
-            def _():
-                copy(*args).wait_send()
+    drain()
+
+    others = norms.at[pl.ds(0, NH - 1)]
+    copy(others, others, n_send, n_recv, at_x(1)).wait()
+    total = jnp.sum(norms[...], axis=0)
+    total = jnp.sum(total, axis=1, keepdims=True)
+    scale = 1.0 / jnp.sqrt(total / float(2 * NX * NZ * TP * 1024) + 1e-6)
+    for t in range(TP):
+        out_ref[pl.ds(t * 16, 8, stride=2), :] = stepv[2 * t] * scale
+        out_ref[pl.ds(t * 16 + 1, 8, stride=2), :] = stepv[2 * t + 1] * scale
+
     assert counts["send"] <= SENDS and counts["recv"] <= RECVS, counts
 
 

time: 38.1 us -> 35.7 us (0.937)
  Pallas kernels: 37.3 us -> 34.9 us
    pallas_call x1, Pallas kernels: 36.5 us -> 34.1 us  [shards(): pl.pallas_call(body, out_shape=(jax.ShapeDtypeStruct((TP * 16, 128), F32)...]
where the time goes in v4:
time: 35.7 us; the launch traced here: 35.6 us
  Pallas kernels  34.9 us (98%)
  between operations  0.64 us (2%)
    pallas_call x1, Pallas kernels, shards(): pl.pallas_call(body, out_shape=(jax.ShapeDtypeStruct((TP * 16, 128), F32)...  34.1 us
    pallas_call x1, Pallas kernels, shards(): pl.pallas_call(finish, out_shape=(jax.ShapeDtypeStruct((TP * 16, 128), F3...  0.8 us

profile of v4, /device:TPU:1, one launch (start us, length us, event | category | flops | bytes accessed | tf_op | source)
XLA Modules:
  0.0 35.6 jit_solution(5499622318110407140)
XLA Ops:
  0.6 34.1 %kadanoff_baym_step.1 = (f32[192,128]{1,0:T(8,128)S(1)}, bf16[2,48,1024]{2,1,0:T(8,128)(2,1)S(1)}) custom-call(f32[192,128]{1,0:T(8,128)} %bitcast.25, f32[192,128]{1,0:T(8,128)} %bitcast.26, f32[32,32]{1,0:T(8,128)} %c_hbm.1, f32[12,32]{1,0:T(8,128)} %damp_hbm.1, f32[12,32]{1,0:T(8,128)} %phase_hbm.1, bf16[2,12,48,1024]{3,2,1,0:T(8,128)(2,1)} %bitcast.22, ...), custom_call_target="tpu_custom_call" | custom-call | tf_op jit(solution)/shard_map/kadanoff_baym_step/pallas_call | solution.py:576
  34.8 0.8 %finish.1 = (f32[192,128]{1,0:T(8,128)}, f32[2,48,1024]{2,1,0:T(8,128)}) custom-call(f32[192,128]{1,0:T(8,128)S(1)} %get-tuple-element.6.step_ref, bf16[2,48,1024]{2,1,0:T(8,128)(2,1)S(1)} %get-tuple-element.7.col_ref), custom_call_target="tpu_custom_call" | custom-call | tf_op jit(solution)/shard_map/finish/pallas_call | solution.py:592

commit v5 on v4

--- a/solution.py
+++ b/solution.py
@@ -288,8 +288,6 @@
                 value = jnp.dot(value, threev[...], preferred_element_type=F32)
                 col_send[c // 2, pl.ds(((c % 2) * 2 + po) * TR, TR), :] = value.astype(BF16)
 
-    for d in FAR_X:
-        start(early, col_send.at[(x + d) % NX], col_x.at[d - 1], cx_send + d - 1, cx_recv + d - 1, at_x(d))
 
     for a, cond in enumerate((jnp.logical_not(source), z > r)):
         for half in range(2):
@@ -298,6 +296,9 @@
                 arrived(sig_own.at[a, pl.ds(0, 32)], z_recv + 2 * a + half)
 
             round_x(a, half, cond)
+
+    for d in FAR_X:
+        start(early, col_send.at[(x + d) % NX], col_x.at[d - 1], cx_send + d - 1, cx_recv + d - 1, at_x(d))
 
     tz_send, tz_recv = slots("send", 7), slots("recv", 7)
     for d in range(1, NX):
@@ -521,8 +522,8 @@
     step.wait()
 
 
-SENDS = 112
-RECVS = 96
+SENDS = 55
+RECVS = 55
 
 
 def shards(row_less, row_great, coupling, damping, phases, lesser_hist, advanced_hist, retarded_hist):

time: 35.7 us -> 35 us (0.980)
  Pallas kernels: 34.9 us -> 34.1 us
    pallas_call x1, Pallas kernels: 34.1 us -> 33.3 us  [shards(): pl.pallas_call(body, out_shape=(jax.ShapeDtypeStruct((TP * 16, 128), F32)...]
where the time goes in v5:
time: 35 us; the launch traced here: 34.7 us
  Pallas kernels  34.1 us (97%)
  between operations  0.64 us (2%)
    pallas_call x1, Pallas kernels, shards(): pl.pallas_call(body, out_shape=(jax.ShapeDtypeStruct((TP * 16, 128), F32)...  33.3 us
    pallas_call x1, Pallas kernels, shards(): pl.pallas_call(finish, out_shape=(jax.ShapeDtypeStruct((TP * 16, 128), F3...  0.8 us

profile of v5, /device:TPU:1, one launch (start us, length us, event | category | flops | bytes accessed | tf_op | source)
XLA Modules:
  0.0 34.7 jit_solution(8374069280979284625)
XLA Ops:
  0.6 33.3 %kadanoff_baym_step.1 = (f32[192,128]{1,0:T(8,128)S(1)}, bf16[2,48,1024]{2,1,0:T(8,128)(2,1)S(1)}) custom-call(f32[192,128]{1,0:T(8,128)} %bitcast.25, f32[192,128]{1,0:T(8,128)} %bitcast.26, f32[32,32]{1,0:T(8,128)} %c_hbm.1, f32[12,32]{1,0:T(8,128)} %damp_hbm.1, f32[12,32]{1,0:T(8,128)} %phase_hbm.1, bf16[2,12,48,1024]{3,2,1,0:T(8,128)(2,1)} %bitcast.22, ...), custom_call_target="tpu_custom_call" | custom-call | tf_op jit(solution)/shard_map/kadanoff_baym_step/pallas_call | solution.py:577
  33.9 0.8 %finish.1 = (f32[192,128]{1,0:T(8,128)}, f32[2,48,1024]{2,1,0:T(8,128)}) custom-call(f32[192,128]{1,0:T(8,128)S(1)} %get-tuple-element.6.step_ref, bf16[2,48,1024]{2,1,0:T(8,128)(2,1)S(1)} %get-tuple-element.7.col_ref), custom_call_target="tpu_custom_call" | custom-call | tf_op jit(solution)/shard_map/finish/pallas_call | solution.py:593

commit v6 on v5

--- a/solution.py
+++ b/solution.py
@@ -68,6 +68,9 @@
     early = z <= r
     source = z == r
     place = (y - z // 2 + 4) % 4 * 2 + (core + z) % 2
+    goes_up = False
+    for k, d in SPREAD.items():
+        goes_up = goes_up | ((place == k) & ((z + d) % NZ > z))
     late = z >= r
 
     def at_x(d):
@@ -106,20 +109,22 @@
             @pl.when(cond)
             def _():
                 copy(*args).start()
-        pending.append((cond, args))
 
     def arrived(ref, recv):
         copy(ref, ref, 0, recv, at_x(1)).wait_recv()
 
     def drain():
-        for cond, args in pending:
+        for cond, ref, send in pending:
             if cond is None:
-                copy(*args).wait_send()
+                copy(ref, ref, send, 0, at_x(1)).wait_send()
             else:
                 @pl.when(cond)
                 def _():
-                    copy(*args).wait_send()
+                    copy(ref, ref, send, 0, at_x(1)).wait_send()
         pending.clear()
+
+    def sent(cond, ref, send):
+        pending.append((cond, ref, send))
 
     loads = []
     for src, dst in (
@@ -200,7 +205,7 @@
 
     pl.semaphore_wait(barrier, (NX - 1) + (NZ - 1) + (NR - 1) + 1)
 
-    z_send, z_recv = slots("send", 4), slots("recv", 4)
+    z_send, z_recv = slots("send", 2), slots("recv", 4)
     for a in range(2):
         for half in range(2):
             rows = pl.ds(32 * half, 32)
@@ -209,7 +214,7 @@
                     continue
                 start(
                     (place == k) if a == 0 else (place == k) & ((z + d) % NZ > z),
-                    sig_own.at[a, rows], sig_all.at[a, x, rows], z_send + 2 * a + half, z_recv + 2 * a + half,
+                    sig_own.at[a, rows], sig_all.at[a, x, rows], z_send + a, z_recv + 2 * a + half,
                     {"hist": (z + d) % NZ * NX + x, "row": z},
                 )
 
@@ -217,13 +222,16 @@
     def _():
         sig_all[:, x] = sig_own[...]
 
-    sx_send, sx_recv = slots("send", 12), slots("recv", 12)
+    sx_send, sx_recv = slots("send", 2), slots("recv", 2)
+    sent(place != 5, sig_own.at[0], z_send)
+    sent((place != 5) & goes_up, sig_own.at[1], z_send + 1)
+    sent(None, sig_all.at[0, pl.ds(0, NX - 1)], sx_send)
+    sent(late, sig_all.at[1, pl.ds(0, NX - 1)], sx_send + 1)
 
     def round_x(a, half, cond):
         block = sig_all.at[a, x, pl.ds(32 * half, 32)]
         for d in FAR_X:
-            at = 6 * a + 3 * half + d - 1
-            start(cond, block, block, sx_send + at, sx_recv + at, at_x(d))
+            start(cond, block, block, sx_send + a, sx_recv + a, at_x(d))
 
     for a in range(2):
         for half in range(2):
@@ -236,9 +244,10 @@
     tot = jnp.concatenate([tot, jnp.zeros((1, 64), F32)], axis=1)
     tot_x[x] = jnp.broadcast_to(tot, (8, 128))
 
-    tx_send, tx_recv = slots("send", 3), slots("recv", 3)
+    tx_send, tx_recv = slots("send", 1), slots("recv", 1)
+    sent(None, tot_z.at[pl.ds(0, NX - 1)], tx_send)
     for d in FAR_X:
-        start(None, tot_x.at[x], tot_x.at[x], tx_send + d - 1, tx_recv + d - 1, at_x(d))
+        start(None, tot_x.at[x], tot_x.at[x], tx_send, tx_recv, at_x(d))
 
     @pl.when(early)
     def _():
@@ -259,7 +268,8 @@
     weight = float(NX * NZ * TP * 32) ** -0.5
     ret_load.wait()
     three_load.wait()
-    cx_send, cx_recv = slots("send", 3), slots("recv", 3)
+    cx_send, cx_recv = slots("send", 1), slots("recv", 1)
+    sent(early, col_x, cx_send)
 
     @pl.when(early)
     def _():
@@ -298,21 +308,22 @@
             round_x(a, half, cond)
 
     for d in FAR_X:
-        start(early, col_send.at[(x + d) % NX], col_x.at[d - 1], cx_send + d - 1, cx_recv + d - 1, at_x(d))
-
-    tz_send, tz_recv = slots("send", 7), slots("recv", 7)
-    for d in range(1, NX):
-        arrived(tot_x.at[0], tx_recv + d - 1)
+        start(early, col_send.at[(x + d) % NX], col_x.at[d - 1], cx_send, cx_recv, at_x(d))
+
+    tz_send, tz_recv = slots("send", 1), slots("recv", 1)
+    sent(None, tot_z.at[pl.ds(0, NZ - 1)], tz_send)
+    arrived(tot_x.at[pl.ds(0, NX - 1)], tx_recv)
     tot_z[z] = tot_x[0] + tot_x[1] + tot_x[2] + tot_x[3]
     for d in FAR_Z:
-        start(None, tot_z.at[z], tot_z.at[z], tz_send + d - 1, tz_recv + d - 1, at_z(d))
-
-    cz_send, cz_recv = slots("send", 7), slots("recv", 7)
+        start(None, tot_z.at[z], tot_z.at[z], tz_send, tz_recv, at_z(d))
+
+    cz_send, cz_recv = slots("send", 1), slots("recv", 7)
+    sent(early & (z < OWNERS), colz_send.at[pl.ds(0, OWNERS - 1)], cz_send)
+    sent(early & (z >= OWNERS), colz_send, cz_send)
 
     @pl.when(early)
     def _():
-        for d in range(1, NX):
-            arrived(col_x.at[d - 1], cx_recv + d - 1)
+        arrived(col_x, cx_recv)
         total = col_send[x].astype(F32)
         for d in range(1, NX):
             total = total + col_x[d - 1].astype(F32)
@@ -322,7 +333,7 @@
     for d in FAR_Z:
         to = (z + d) % NZ
         start(
-            early & (to < OWNERS), colz_send.at[lax.rem(to, OWNERS)], col_z.at[d - 1], cz_send + d - 1, cz_recv + d - 1, at_z(d)
+            early & (to < OWNERS), colz_send.at[lax.rem(to, OWNERS)], col_z.at[d - 1], cz_send, cz_recv + d - 1, at_z(d)
         )
 
     one_load.wait()
@@ -381,9 +392,7 @@
         lax.fori_loop(0, TP // 4, step, 0, unroll=True)
 
     les_load.wait()
-    for d in range(1, NX):
-        for half in range(2):
-            arrived(sig_own.at[0, pl.ds(0, 32)], sx_recv + 3 * half + d - 1)
+    arrived(sig_all.at[0, pl.ds(0, NX - 1)], sx_recv)
     left_matrix(0)
     contract(lesv, False, 1 - core)
     contract(lesv, False, core)
@@ -391,13 +400,12 @@
 
     @pl.when(late)
     def _():
-        for d in range(1, NX):
-            for half in range(2):
-                arrived(sig_own.at[1, pl.ds(0, 32)], sx_recv + 6 + 3 * half + d - 1)
+        arrived(sig_all.at[1, pl.ds(0, NX - 1)], sx_recv + 1)
         left_matrix(1)
         contract(advv, True, 1 - core)
 
     rc_send, rc_recv = slots("send", 1), slots("recv", 1)
+    sent(None, rs_buf, rc_send)
     start(None, fpart.at[pl.ds(TP * (1 - core), TP)], rs_buf, rc_send, rc_recv, at_core())
 
     @pl.when(late)
@@ -405,14 +413,16 @@
         contract(advv, True, core)
 
     arrived(rs_buf, rc_recv)
-    ry_send, ry_recv = slots("send", 7), slots("recv", 7)
+    ry_send, ry_recv = slots("send", 1), slots("recv", 1)
+    sent(None, y_buf.at[pl.ds(0, NR - 1)], ry_send)
     half = fpart[pl.ds(TP * core, TP)] + rs_buf[...]
     y_buf[r] = half.reshape(TP * 8, 128).astype(BF16)
     for d in FAR_R:
-        start(None, y_buf.at[r], y_buf.at[r], ry_send + d - 1, ry_recv + d - 1, at_r(d))
-
-    cg_send, cg_recv = slots("send", 7), slots("recv", 7)
+        start(None, y_buf.at[r], y_buf.at[r], ry_send, ry_recv, at_r(d))
+
+    cg_send, cg_recv = slots("send", 1), slots("recv", 1)
     owner = z < OWNERS
+    sent(owner, fpart.at[pl.ds(0, 14)], cg_send)
 
     @pl.when(owner)
     def _():
@@ -434,10 +444,9 @@
 
     piece = col_all.at[x, lax.rem(z, OWNERS)]
     for d in FAR_Z:
-        start(owner, piece, piece, cg_send + d - 1, cg_recv + d - 1, at_z(d))
-
-    for d in range(1, NZ):
-        arrived(tot_z.at[0], tz_recv + d - 1)
+        start(owner, piece, piece, cg_send, cg_recv, at_z(d))
+
+    arrived(tot_z.at[pl.ds(0, NZ - 1)], tz_recv)
     above = jnp.zeros((8, 128), F32)
     for j in range(NZ):
         above = above + jnp.where(j > z, tot_z[j], 0.0)
@@ -456,8 +465,7 @@
     for c in range(8):
         facv[pl.ds(c, 2 * TP, stride=8), :] = spread[:, c * 128 : c * 128 + 128]
 
-    for d in range(1, NR):
-        arrived(y_buf.at[0], ry_recv + d - 1)
+    arrived(y_buf.at[pl.ds(0, NR - 1)], ry_recv)
     halves = []
     for k in range(2):
         half = y_buf[k].astype(F32)
@@ -479,16 +487,20 @@
     for d in FAR_H:
         copy(norms.at[h], norms.at[h], n_send, n_recv, at_h(d)).start()
 
-    ca_send, ca_recv = slots("send", 3), slots("recv", 3)
-    for d in range(1, NZ):
-        @pl.when((z - d + NZ) % NZ < OWNERS)
-        def _():
-            arrived(col_all.at[0, 0], cg_recv + d - 1)
+    ca_send, ca_recv = slots("send", 1), slots("recv", 1)
+    sent(None, col_all.at[pl.ds(0, NX - 1)], ca_send)
+    @pl.when(owner)
+    def _():
+        arrived(col_all.at[0, pl.ds(0, OWNERS - 1)], cg_recv)
+
+    @pl.when(jnp.logical_not(owner))
+    def _():
+        arrived(col_all.at[0], cg_recv)
+
     for d in FAR_X:
-        start(None, col_all.at[x], col_all.at[x], ca_send + d - 1, ca_recv + d - 1, at_x(d))
-
-    for d in range(1, NX):
-        arrived(col_all.at[0], ca_recv + d - 1)
+        start(None, col_all.at[x], col_all.at[x], ca_send, ca_recv, at_x(d))
+
+    arrived(col_all.at[pl.ds(0, NX - 1)], ca_recv)
     for j in range(NX):
         rows = col_all[j].reshape(4 * TR, 128)
         for c in range(2):
@@ -522,8 +534,8 @@
     step.wait()
 
 
-SENDS = 55
-RECVS = 55
+SENDS = 13
+RECVS = 21
 
 
 def shards(row_less, row_great, coupling, damping, phases, lesser_hist, advanced_hist, retarded_hist):

time: 35 us -> 34.3 us (0.980)
  Pallas kernels: 34.1 us -> 33.4 us
    pallas_call x1, Pallas kernels: 33.3 us -> 32.6 us  [shards(): pl.pallas_call(body, out_shape=(jax.ShapeDtypeStruct((TP * 16, 128), F32)...]
where the time goes in v6:
time: 34.3 us; the launch traced here: 34.1 us
  Pallas kernels  33.4 us (97%)
  between operations  0.64 us (2%)
    pallas_call x1, Pallas kernels, shards(): pl.pallas_call(body, out_shape=(jax.ShapeDtypeStruct((TP * 16, 128), F32)...  32.6 us
    pallas_call x1, Pallas kernels, shards(): pl.pallas_call(finish, out_shape=(jax.ShapeDtypeStruct((TP * 16, 128), F3...  0.8 us

profile of v6, /device:TPU:1, one launch (start us, length us, event | category | flops | bytes accessed | tf_op | source)
XLA Modules:
  0.0 34.1 jit_solution(5983838014986004611)
XLA Ops:
  0.6 32.6 %kadanoff_baym_step.1 = (f32[192,128]{1,0:T(8,128)S(1)}, bf16[2,48,1024]{2,1,0:T(8,128)(2,1)S(1)}) custom-call(f32[192,128]{1,0:T(8,128)} %bitcast.25, f32[192,128]{1,0:T(8,128)} %bitcast.26, f32[32,32]{1,0:T(8,128)} %c_hbm.1, f32[12,32]{1,0:T(8,128)} %damp_hbm.1, f32[12,32]{1,0:T(8,128)} %phase_hbm.1, bf16[2,12,48,1024]{3,2,1,0:T(8,128)(2,1)} %bitcast.22, ...), custom_call_target="tpu_custom_call" | custom-call | tf_op jit(solution)/shard_map/kadanoff_baym_step/pallas_call | solution.py:589
  33.2 0.8 %finish.1 = (f32[192,128]{1,0:T(8,128)}, f32[2,48,1024]{2,1,0:T(8,128)}) custom-call(f32[192,128]{1,0:T(8,128)S(1)} %get-tuple-element.6.step_ref, bf16[2,48,1024]{2,1,0:T(8,128)(2,1)S(1)} %get-tuple-element.7.col_ref), custom_call_target="tpu_custom_call" | custom-call | tf_op jit(solution)/shard_map/finish/pallas_call | solution.py:605
